TPU v7x, 256 devices: a whole 4x4x8 slice. The times are simulated.
256 devices in a mesh: grp: 8 (over x, y_hi), blk: 32 (over y_lo, z, core).
Axes of the slice: x: 4, y: 4 (y_hi: 2, y_lo: 2; y = y_hi * 2 + y_lo), z: 8, core: 2. Of those that a mesh axis runs over, the one named last changes fastest.
Arguments:
- amplitudes: float32 [8192, 1176], P(('grp', 'blk')), may hold values from -6 to 6
- integrals: float32 [8192, 65536], P(('grp', 'blk')), may hold values from -0.0625 to 0.0625
Outputs:
- ladder: float32 [1176, 65536], P('grp', 'blk')
All inputs are finite; a program needn't handle non-finite values.
Results may differ from a plain program's by a relative error of at most 0.00007.
Values sent between devices are 32-bit elements; how exact they have to be, the bound alone decides.
No kernel may reach another device: no remote copies, remote signals or barrier semaphores. Data moves between devices by JAX's collectives and lax.ppermute only.
A program may use at most 128 MiB of HBM per device.

v0:
```python
import jax
import jax.numpy as jnp
from jax import lax
from jax.experimental import pallas as pl
from jax.experimental.pallas import tpu as pltpu
from jax.sharding import Mesh, PartitionSpec as P

AXES = ("x", "yh", "yl", "z", "c")
PLANE = ("x", "yh", "yl", "c")
NZ = 8
IJ, ROWS = 1176, 147
HALF = 640
CHUNKS = ((4,), (3, -3), (2, -2), (1, -1), (0,))
SMALL = pltpu.CompilerParams(vmem_limit_bytes=16 * 2**20)
BIG = pltpu.CompilerParams(vmem_limit_bytes=56 * 2**20)


def pack_kernel(n, blocks_ref, *refs):
    for k in range(n):
        for c in range(2):
            for s in range(8):
                start = c * 2048 + s * 256
                refs[-1 if len(refs) == n + 1 else n + 1][
                    s, c, :, k * 256 : (k + 1) * 256
                ] = refs[k][:, start : start + 256]
    if len(refs) == n + 1:
        return
    amps_ref, out_ref, wide = refs[n:]
    wide[:, 1152:] = jnp.zeros((wide.shape[0], 128), jnp.float32)
    wide[:, :IJ] = amps_ref[...]
    for c in range(2):
        for s in range(8):
            out_ref[s, c, :, n * 256 :] = wide[:, c * HALF : (c + 1) * HALF]


def pack(integrals, blocks, n, amplitudes=None):
    rows = integrals.shape[0]
    width = n * 256 + (0 if amplitudes is None else HALF)
    specs = [
        pl.BlockSpec((rows, 4096), lambda y, b, k=k: (0, y * NZ + b[k])) for k in range(n)
    ]
    extra, scratch = [], []
    if amplitudes is not None:
        specs.append(pl.BlockSpec((rows, IJ), lambda y, b: (0, 0)))
        extra.append(amplitudes)
        scratch.append(pltpu.VMEM((rows, 2 * HALF), jnp.float32))
    out = pl.pallas_call(
        lambda *refs: pack_kernel(n, *refs),
        out_shape=jax.ShapeDtypeStruct((8, 4, rows, width), jnp.float32),
        grid_spec=pltpu.PrefetchScalarGridSpec(
            num_scalar_prefetch=1,
            grid=(2,),
            in_specs=specs,
            out_specs=pl.BlockSpec((8, 2, rows, width), lambda y, b: (0, y, 0, 0)),
            scratch_shapes=scratch,
        ),
        compiler_params=BIG,
        cost_estimate=pl.CostEstimate(
            flops=0, bytes_accessed=64 * rows * width * 4, transcendentals=0
        ),
        name="pack",
    )(blocks, *[integrals] * n, *extra)
    return out.reshape(32, rows, width)


def prepare_kernel(in_ref, high_ref, low_ref):
    value = (0.5 * in_ref[...]).T
    high = value.astype(jnp.bfloat16)
    high_ref[...] = high
    low_ref[...] = (value - high.astype(jnp.float32)).astype(jnp.bfloat16)


def prepare(slab, first):
    depth = slab.shape[0]
    half = jax.ShapeDtypeStruct((HALF, depth), jnp.bfloat16)
    spec = pl.BlockSpec((128, depth), lambda k: (k, 0))
    return pl.pallas_call(
        prepare_kernel,
        out_shape=(half, half),
        grid=(HALF // 128,),
        in_specs=[pl.BlockSpec((depth, 128), lambda k: (0, first + k))],
        out_specs=(spec, spec),
        compiler_params=SMALL,
        cost_estimate=pl.CostEstimate(
            flops=0, bytes_accessed=depth * HALF * 8, transcendentals=0
        ),
        name="prepare",
    )(slab)


def first_kernel(amps_ref, v_ref, out_ref):
    def split(value):
        high = value.astype(jnp.bfloat16)
        return high, (value - high.astype(jnp.float32)).astype(jnp.bfloat16)

    def dot(left_side, right_side):
        return lax.dot_general(
            left_side,
            right_side,
            (((0,), (0,)), ((), ())),
            preferred_element_type=jnp.float32,
        )

    th, tl = split(0.5 * amps_ref[...])
    vh, vl = split(v_ref[...])
    out_ref[...] = dot(tl, vh) + dot(th, vl) + dot(th, vh)


def first(amps, slab):
    depth = amps.shape[0]
    return pl.pallas_call(
        first_kernel,
        out_shape=jax.ShapeDtypeStruct((HALF, 256), jnp.float32),
        grid=(1,),
        in_specs=[
            pl.BlockSpec((depth, HALF), lambda k: (0, 0)),
            pl.BlockSpec((depth, 256), lambda k: (0, 0)),
        ],
        out_specs=pl.BlockSpec((HALF, 256), lambda k: (0, 0)),
        compiler_params=SMALL,
        cost_estimate=pl.CostEstimate(
            flops=6 * HALF * depth * 256,
            bytes_accessed=4 * depth * (HALF + 256) + HALF * 1024,
            transcendentals=0,
        ),
        name="first",
    )(amps, slab)


def product_kernel(n, core_ref, ha_ref, la_ref, hb_ref, lb_ref, v_ref, *refs):
    outs, sums = refs[-2 - n : -2], refs[: -2 - n]
    vh, vl = refs[-2:]
    step = pl.program_id(0)

    @pl.when(step == 0)
    def _():
        piece = v_ref[...]
        high = piece.astype(jnp.bfloat16)
        vh[...] = high
        vl[...] = (piece - high.astype(jnp.float32)).astype(jnp.bfloat16)

    def dot(left_side, right_side):
        return jnp.dot(left_side, right_side, preferred_element_type=jnp.float32)

    def rows(h_ref, l_ref, gets_sum):
        value = dot(l_ref[...], vh[...]) + dot(h_ref[...], vl[...])
        value += dot(h_ref[...], vh[...])
        for k in range(n):
            block = value[:, k * 256 : (k + 1) * 256]
            outs[k][...] = block + sums[k][...] if sums and k == gets_sum else block

    pl.when(step < 2)(lambda: rows(ha_ref, la_ref, 0))
    pl.when(step >= 2)(lambda: rows(hb_ref, lb_ref, 1))


def contract(core, amps, slab, n, sums=()):
    depth = slab.shape[0]

    def own(m):
        return jnp.minimum(m, 1)

    def other(m):
        return jnp.maximum(m - 2, 0)

    def place(m, core):
        return jnp.where(m < 2, core[0] * 2 + m, (1 - core[0]) * 2 + m - 2), 0

    return pl.pallas_call(
        lambda *refs: product_kernel(n, *refs),
        out_shape=[jax.ShapeDtypeStruct((IJ, 256), jnp.float32)] * n,
        grid_spec=pltpu.PrefetchScalarGridSpec(
            num_scalar_prefetch=1,
            grid=(4,),
            in_specs=[pl.BlockSpec((320, depth), lambda m, c: (own(m), 0))] * 2
            + [pl.BlockSpec((320, depth), lambda m, c: (other(m), 0))] * 2
            + [pl.BlockSpec((depth, n * 256), lambda m, c: (0, 0))]
            + [
                pl.BlockSpec((320, 256), lambda m, c: (own(m), 0)),
                pl.BlockSpec((320, 256), lambda m, c: (other(m), 0)),
            ][: len(sums)],
            out_specs=[pl.BlockSpec((320, 256), place)] * n,
            scratch_shapes=[pltpu.VMEM((depth, n * 256), jnp.bfloat16)] * 2,
        ),
        compiler_params=BIG,
        cost_estimate=pl.CostEstimate(
            flops=6 * n * IJ * depth * 256,
            bytes_accessed=8 * depth * HALF + n * (depth + IJ) * 1024,
            transcendentals=0,
        ),
        name="product",
    )(core, *amps, slab, *sums)


def on_device(amplitudes, integrals):
    rows = integrals.shape[0]
    z = lax.axis_index("z")
    core = lax.axis_index("c").astype(jnp.int32).reshape(1)
    up = [(i, (i + 1) % NZ) for i in range(NZ)]
    down = [(i, (i - 1) % NZ) for i in range(NZ)]

    def swap(sent):
        got = lax.all_to_all(sent, PLANE, split_axis=0, concat_axis=0, tiled=True)
        return got.reshape(32 * rows, -1)

    sent = []
    for place, offsets in enumerate(CHUNKS):
        blocks = ((z + jnp.array(offsets, jnp.int32) + NZ) % NZ).astype(jnp.int32)
        sent.append(pack(integrals, blocks, len(offsets), None if place else amplitudes))

    slab = swap(sent[0])
    slab, *sent[1:] = lax.optimization_barrier((slab, *sent[1:]))
    width = len(CHUNKS[0]) * 256
    own = slab[:, width:]
    other = lax.ppermute(own, "c", [(0, 1), (1, 0)])
    right, left = first(own, slab), first(other, slab)
    own, other, right, left = lax.optimization_barrier((own, other, right, left))
    amps = (*prepare(own, 0), *prepare(other, 0))

    for place in range(1, 4):
        right = lax.ppermute(right, "z", up)
        left = lax.ppermute(left, "z", down)
        slab = swap(sent[place])
        if place == 1:
            right, left, slab, sent[2], *amps = lax.optimization_barrier(
                (right, left, slab, sent[2], *amps)
            )
            right, left = contract(core, amps, slab, 2, (right, left))
            continue
        ups, downs = contract(core, amps, slab, 2)
        right, left = right + ups, left + downs
    right = lax.ppermute(right, "z", up)
    left = lax.ppermute(left, "z", down)
    own = contract(core, amps, swap(sent[4]), 1)[0]
    total = (own + right + left).reshape(8, ROWS, 256)
    got = lax.all_to_all(total, ("x", "yh"), split_axis=0, concat_axis=0, tiled=True)
    return got.transpose(1, 0, 2).reshape(ROWS, 8 * 256)


def solution(mesh):
    fine = Mesh(mesh.devices.reshape(4, 2, 2, NZ, 2), AXES)
    return jax.shard_map(
        on_device,
        mesh=fine,
        in_specs=(P(AXES, None), P(AXES, None)),
        out_specs=P(("x", "yh"), ("yl", "z", "c")),
        check_vma=False,
    )
```

profile of v0, /device:TPU:102, one launch (start us, length us, event | category | flops | bytes accessed | tf_op | source)
XLA Modules:
  0.0 236.3 jit_solution(4847326841388640016)
XLA Ops:
  0.0 3.0 %pack.5 = f32[8,4,32,896]{3,2,1,0:T(8,128)} custom-call(s32[1]{0:T(128)S(6)} %select_n.25.refs_0_, f32[32,65536]{1,0:T(8,128)} %refs_1_.9, f32[32,1176]{1,0:T(8,128)} %refs_2_.4), custom_call_target="tpu_custom_call" | custom-call | bytes 7340032 | tf_op jit(solution)/shard_map/pack/pallas_call | solution.py:47
  3.0 7.7 %all-to-all-start = ((f32[32,32,896]{2,1,0:T(8,128)}), f32[32,32,896]{2,1,0:T(8,128)}, u32[]{:S(2)}, u32[]{:S(2)}) async-start(f32[32,32,896]{2,1,0:T(8,128)} %bitcast.17), calls=%async_computation | async-start | bytes 7340032 | tf_op jit(solution)/shard_map/all_to_all | solution.py:202
  10.7 2.1 pack.9
  12.8 0.6 and_select_fusion
  13.4 3.5 %pack.8 = f32[8,4,32,512]{3,2,1,0:T(8,128)} custom-call(s32[2]{0:T(128)} %get-tuple-element.59.refs_0_, f32[32,65536]{1,0:T(8,128)} %refs_1_.9, f32[32,65536]{1,0:T(8,128)} %refs_1_.9), custom_call_target="tpu_custom_call" | custom-call | bytes 4194304 | tf_op jit(solution)/shard_map/pack/pallas_call | solution.py:47
  16.9 0.5 and_select_fusion.2.refs_0_
  17.5 3.4 %pack.6 = f32[8,4,32,512]{3,2,1,0:T(8,128)} custom-call(s32[2]{0:T(128)} %and_select_fusion.2.refs_0_, f32[32,65536]{1,0:T(8,128)} %refs_1_.9, f32[32,65536]{1,0:T(8,128)} %refs_1_.9), custom_call_target="tpu_custom_call" | custom-call | bytes 4194304 | tf_op jit(solution)/shard_map/pack/pallas_call | solution.py:47
  20.8 3.3 %pack.7 = f32[8,4,32,512]{3,2,1,0:T(8,128)} custom-call(s32[2]{0:T(128)} %get-tuple-element.60.refs_0_, f32[32,65536]{1,0:T(8,128)} %refs_1_.9, f32[32,65536]{1,0:T(8,128)} %refs_1_.9), custom_call_target="tpu_custom_call" | custom-call | bytes 4194304 | tf_op jit(solution)/shard_map/pack/pallas_call | solution.py:47
  24.1 31.3 %all-to-all-done = f32[32,32,896]{2,1,0:T(8,128)} async-done(((f32[32,32,896]{2,1,0:T(8,128)}), f32[32,32,896]{2,1,0:T(8,128)}, u32[]{:S(2)}, u32[]{:S(2)}) %all-to-all-start) | async-done | bytes 3670048 | tf_op jit(solution)/shard_map/all_to_all | solution.py:202
  55.4 1.9 slice.3.amps_ref.in_ref
  57.4 8.2 %all-to-all-start.1 = ((f32[32,32,512]{2,1,0:T(8,128)}), f32[32,32,512]{2,1,0:T(8,128)}, u32[]{:S(2)}, u32[]{:S(2)}) async-start(f32[32,32,512]{2,1,0:T(8,128)} %bitcast.18), calls=%async_computation.1 | async-start | bytes 4194304 | tf_op jit(solution)/shard_map/all_to_all | solution.py:202
  65.6 2.5 %first.2 = f32[640,256]{1,0:T(8,128)S(1)} custom-call(f32[1024,640]{1,0:T(8,128)S(1)} %slice.3.amps_ref.in_ref, f32[1024,896]{1,0:T(8,128)} %bitcast.3.v_ref), custom_call_target="tpu_custom_call" | custom-call | flops 1006632960 | bytes 4325376 | tf_op jit(solution)/shard_map/first/pallas_call | solution.py:111
  68.1 4.1 %first.3 = f32[640,256]{1,0:T(8,128)} custom-call(f32[1024,640]{1,0:T(8,128)} %collective-permute-done.amps_ref.in_ref, f32[1024,896]{1,0:T(8,128)} %bitcast.3.v_ref), custom_call_target="tpu_custom_call" | custom-call | flops 1006632960 | bytes 4325376 | tf_op jit(solution)/shard_map/first/pallas_call | solution.py:111
  72.2 3.1 %collective-permute-start.1 = (f32[640,256]{1,0:T(8,128)S(1)}, f32[640,256]{1,0:T(8,128)}, u32[]{:S(2)}, u32[]{:S(2)}) collective-permute-start(f32[640,256]{1,0:T(8,128)S(1)} %first.2), channel_id=1, source_target_pairs={{0,2},{2,4},{4,6},{6,8},{8,10},{10,12},{12,14},{14,0},{1,3},{3,5},... | collective-permute-start | bytes 1966088 | tf_op jit(solution)/shard_map/ppermute | solution.py:220
  75.3 1.3 prepare.2
  76.6 1.1 copy-done
  77.7 1.1 copy-done.1
  78.7 3.8 %prepare.3 = (bf16[640,1024]{1,0:T(8,128)(2,1)S(1)}, bf16[640,1024]{1,0:T(8,128)(2,1)S(1)}) custom-call(f32[1024,640]{1,0:T(8,128)} %collective-permute-done.amps_ref.in_ref), custom_call_target="tpu_custom_call" | custom-call | bytes 5242880 | tf_op jit(solution)/shard_map/prepare/pallas_call | solution.py:77
  82.5 1.1 copy-done.2
  83.6 1.1 copy-done.3
  84.7 7.3 %all-to-all-done.1 = f32[32,32,512]{2,1,0:T(8,128)} async-done(((f32[32,32,512]{2,1,0:T(8,128)}), f32[32,32,512]{2,1,0:T(8,128)}, u32[]{:S(2)}, u32[]{:S(2)}) %all-to-all-start.1) | async-done | bytes 2097184 | tf_op jit(solution)/shard_map/all_to_all | solution.py:202
  92.0 1.4 collective-permute-done.2.refs_7_
  93.4 7.4 %all-to-all-start.3 = ((f32[32,32,512]{2,1,0:T(8,128)}), f32[32,32,512]{2,1,0:T(8,128)S(1)}, u32[]{:S(2)}, u32[]{:S(2)}) async-start(f32[32,32,512]{2,1,0:T(8,128)} %bitcast.5), calls=%async_computation.3 | async-start | bytes 4194304 | tf_op jit(solution)/shard_map/all_to_all | solution.py:202
  100.8 9.2 %product.5 = (f32[1176,256]{1,0:T(8,128)}, f32[1176,256]{1,0:T(8,128)}) custom-call(s32[1]{0:T(128)} %bitcast.refs_0_, bf16[640,1024]{1,0:T(8,128)(2,1)} %copy-done, bf16[640,1024]{1,0:T(8,128)(2,1)} %copy-done.1, bf16[640,1024]{1,0:T(8,128)(2,1)} %copy-done.2, bf16[640,1024]{1,0:T(8,128)(2,1)} %copy-done.3, f32[1024,512]{1,0:T(8,128)} %bitcast.9.refs_5_, ...), custom_call_target="tpu_custom_call" | custom-call | flops 3699376128 | bytes 9748480 | tf_op jit(solution)/shard_map/product/pallas_call | solution.py:168
  110.0 1.0 collective-permute-start.3
  110.9 1.0 collective-permute-start.6
  112.0 15.1 %all-to-all-done.3 = f32[32,32,512]{2,1,0:T(8,128)S(1)} async-done(((f32[32,32,512]{2,1,0:T(8,128)}), f32[32,32,512]{2,1,0:T(8,128)S(1)}, u32[]{:S(2)}, u32[]{:S(2)}) %all-to-all-start.3) | async-done | bytes 2097184 | tf_op jit(solution)/shard_map/all_to_all | solution.py:202
  127.1 1.3 copy-done.6
  128.4 6.6 %all-to-all-start.4 = ((f32[32,32,512]{2,1,0:T(8,128)}), f32[32,32,512]{2,1,0:T(8,128)S(1)}, u32[]{:S(2)}, u32[]{:S(2)}) async-start(f32[32,32,512]{2,1,0:T(8,128)} %bitcast.6), calls=%async_computation.4 | async-start | bytes 4194304 | tf_op jit(solution)/shard_map/all_to_all | solution.py:202
  135.1 9.1 %product.6 = (f32[1176,256]{1,0:T(8,128)}, f32[1176,256]{1,0:T(8,128)}) custom-call(s32[1]{0:T(128)} %bitcast.refs_0_, bf16[640,1024]{1,0:T(8,128)(2,1)} %copy-done, bf16[640,1024]{1,0:T(8,128)(2,1)} %copy-done.1, bf16[640,1024]{1,0:T(8,128)(2,1)} %copy-done.2, bf16[640,1024]{1,0:T(8,128)(2,1)} %copy-done.3, f32[1024,512]{1,0:T(8,128)} %bitcast.24), custom_call_target="tpu_custom_call" | custom-call | flops 3699376128 | bytes 9748480 | tf_op jit(solution)/shard_map/product/pallas_call | solution.py:168
  144.2 2.9 %add.98 = f32[1176,256]{1,0:T(8,128)} add(f32[1176,256]{1,0:T(8,128)} %collective-permute-done.3, f32[1176,256]{1,0:T(8,128)} %get-tuple-element.53) | non-fusion elementwise | flops 301056 | bytes 3612672 | tf_op jit(solution)/shard_map/add | solution.py:230
  147.1 1.0 collective-permute-start.4
  148.1 1.2 add.101
  149.2 1.1 collective-permute-start.7
  150.3 11.1 %all-to-all-done.4 = f32[32,32,512]{2,1,0:T(8,128)S(1)} async-done(((f32[32,32,512]{2,1,0:T(8,128)}), f32[32,32,512]{2,1,0:T(8,128)S(1)}, u32[]{:S(2)}, u32[]{:S(2)}) %all-to-all-start.4) | async-done | bytes 2097184 | tf_op jit(solution)/shard_map/all_to_all | solution.py:202
  161.4 1.3 copy-done.5
  162.7 9.1 %product.7 = (f32[1176,256]{1,0:T(8,128)}, f32[1176,256]{1,0:T(8,128)}) custom-call(s32[1]{0:T(128)} %bitcast.refs_0_, bf16[640,1024]{1,0:T(8,128)(2,1)} %copy-done, bf16[640,1024]{1,0:T(8,128)(2,1)} %copy-done.1, bf16[640,1024]{1,0:T(8,128)(2,1)} %copy-done.2, bf16[640,1024]{1,0:T(8,128)(2,1)} %copy-done.3, f32[1024,512]{1,0:T(8,128)} %bitcast.23), custom_call_target="tpu_custom_call" | custom-call | flops 3699376128 | bytes 9748480 | tf_op jit(solution)/shard_map/product/pallas_call | solution.py:168
  171.8 4.2 %collective-permute-done.4 = f32[1176,256]{1,0:T(8,128)} collective-permute-done((f32[1176,256]{1,0:T(8,128)}, f32[1176,256]{1,0:T(8,128)}, u32[]{:S(2)}, u32[]{:S(2)}) %collective-permute-start.4) | collective-permute-done | bytes 1204256 | tf_op jit(solution)/shard_map/ppermute | solution.py:220
  176.0 1.9 add.99
  177.9 2.2 collective-permute-start.5
  180.1 0.2 add.102
  180.4 1.0 copy-done.4
  181.4 22.5 %all_to_all.30 = f32[32,32,256]{2,1,0:T(8,128)} all-to-all(f32[32,32,256]{2,1,0:T(8,128)S(1)} %bitcast.21), channel_id=1, replica_groups=mesh['x'=4,'yh'=2,'yl'=2,'z'=8,'c'=2] {'x','yh','yl','c'}, dimensions={0} | all-to-all | bytes 2097152 | tf_op jit(solution)/shard_map/all_to_all | solution.py:202
  203.9 6.6 %product.4 = f32[1176,256]{1,0:T(8,128)} custom-call(s32[1]{0:T(128)} %bitcast.refs_0_, bf16[640,1024]{1,0:T(8,128)(2,1)} %copy-done, bf16[640,1024]{1,0:T(8,128)(2,1)} %copy-done.1, bf16[640,1024]{1,0:T(8,128)(2,1)} %copy-done.2, bf16[640,1024]{1,0:T(8,128)(2,1)} %copy-done.3, f32[1024,256]{1,0:T(8,128)} %bitcast.22), custom_call_target="tpu_custom_call" | custom-call | flops 1849688064 | bytes 7495680 | tf_op jit(solution)/shard_map/product/pallas_call | solution.py:168
  210.5 1.5 add_add_fusion
  212.2 22.2 %all_to_all.31 = f32[8,147,256]{2,1,0:T(8,128)S(1)} all-to-all(f32[8,147,256]{2,1,0:T(8,128)S(1)} %reshape.54), channel_id=1, replica_groups=mesh['x'=4,'yh'=2,'yl'=2,'z'=8,'c'=2] {'x','yh'}, dimensions={0} | all-to-all | bytes 2408448 | tf_op jit(solution)/shard_map/all_to_all | solution.py:235
  234.4 0.4 copy.9
  234.9 1.5 copy.10
  (29 shorter events, 0.5 us)
Async XLA Ops:
  3.0 52.4 %all-to-all-start = ((f32[32,32,896]{2,1,0:T(8,128)}), f32[32,32,896]{2,1,0:T(8,128)}, u32[]{:S(2)}, u32[]{:S(2)}) async-start(f32[32,32,896]{2,1,0:T(8,128)} %bitcast.17), calls=%async_computation | async-start | bytes 7340032 | tf_op jit(solution)/shard_map/all_to_all | solution.py:202
  10.7 2.1 copy-start.9
  10.7 2.1 copy-start.10
  13.4 3.5 %copy-start.11 = (s32[2]{0:T(128)S(1)}, s32[2]{0:T(128)}, u32[]{:S(2)}) copy-start(s32[2]{0:T(128)} %constant.68.clone) | copy-start | bytes 28
  57.3 10.8 %collective-permute-start = (f32[1024,640]{1,0:T(8,128)S(1)}, f32[1024,640]{1,0:T(8,128)}, u32[]{:S(2)}, u32[]{:S(2)}) collective-permute-start(f32[1024,640]{1,0:T(8,128)S(1)} %slice.3.amps_ref.in_ref), channel_id=1, source_target_pairs={{0,1},{1,0},{2,3},{3,2},{4,5},{5,4},{6,7},{7,6},{8,9},{9,8},{10,11... | collective-permute-start | bytes 7864328 | tf_op jit(solution)/shard_map/ppermute | solution.py:214
  57.4 34.6 %all-to-all-start.1 = ((f32[32,32,512]{2,1,0:T(8,128)}), f32[32,32,512]{2,1,0:T(8,128)}, u32[]{:S(2)}, u32[]{:S(2)}) async-start(f32[32,32,512]{2,1,0:T(8,128)} %bitcast.18), calls=%async_computation.1 | async-start | bytes 4194304 | tf_op jit(solution)/shard_map/all_to_all | solution.py:202
  72.2 19.8 %collective-permute-start.1 = (f32[640,256]{1,0:T(8,128)S(1)}, f32[640,256]{1,0:T(8,128)}, u32[]{:S(2)}, u32[]{:S(2)}) collective-permute-start(f32[640,256]{1,0:T(8,128)S(1)} %first.2), channel_id=1, source_target_pairs={{0,2},{2,4},{4,6},{6,8},{8,10},{10,12},{12,14},{14,0},{1,3},{3,5},... | collective-permute-start | bytes 1966088 | tf_op jit(solution)/shard_map/ppermute | solution.py:220
  75.3 18.0 %collective-permute-start.2 = (f32[640,256]{1,0:T(8,128)}, f32[640,256]{1,0:T(8,128)}, u32[]{:S(2)}, u32[]{:S(2)}) collective-permute-start(f32[640,256]{1,0:T(8,128)} %first.3), channel_id=1, source_target_pairs={{0,14},{2,0},{4,2},{6,4},{8,6},{10,8},{12,10},{14,12},{1,15},{3,1}... | collective-permute-start | bytes 1966088 | tf_op jit(solution)/shard_map/ppermute | solution.py:221
  76.6 1.1 copy-start
  77.7 1.1 copy-start.1
  82.5 1.1 copy-start.2
  83.6 1.1 copy-start.3
  93.4 33.7 %all-to-all-start.3 = ((f32[32,32,512]{2,1,0:T(8,128)}), f32[32,32,512]{2,1,0:T(8,128)S(1)}, u32[]{:S(2)}, u32[]{:S(2)}) async-start(f32[32,32,512]{2,1,0:T(8,128)} %bitcast.5), calls=%async_computation.3 | async-start | bytes 4194304 | tf_op jit(solution)/shard_map/all_to_all | solution.py:202
  110.0 34.2 %collective-permute-start.3 = (f32[1176,256]{1,0:T(8,128)}, f32[1176,256]{1,0:T(8,128)}, u32[]{:S(2)}, u32[]{:S(2)}) collective-permute-start(f32[1176,256]{1,0:T(8,128)} %get-tuple-element.51), channel_id=1, source_target_pairs={{0,2},{2,4},{4,6},{6,8},{8,10},{10,12},{12,14},{14,0},{1,3},{3,5},... | collective-permute-start | bytes 3612680 | tf_op jit(solution)/shard_map/ppermute | solution.py:220
  110.9 37.1 %collective-permute-start.6 = (f32[1176,256]{1,0:T(8,128)}, f32[1176,256]{1,0:T(8,128)S(1)}, u32[]{:S(2)}, u32[]{:S(2)}) collective-permute-start(f32[1176,256]{1,0:T(8,128)} %get-tuple-element.56), channel_id=1, source_target_pairs={{0,14},{2,0},{4,2},{6,4},{8,6},{10,8},{12,10},{14,12},{1,15},{3,1}... | collective-permute-start | bytes 3612680 | tf_op jit(solution)/shard_map/ppermute | solution.py:221
  127.1 1.4 copy-start.6
  128.4 32.9 %all-to-all-start.4 = ((f32[32,32,512]{2,1,0:T(8,128)}), f32[32,32,512]{2,1,0:T(8,128)S(1)}, u32[]{:S(2)}, u32[]{:S(2)}) async-start(f32[32,32,512]{2,1,0:T(8,128)} %bitcast.6), calls=%async_computation.4 | async-start | bytes 4194304 | tf_op jit(solution)/shard_map/all_to_all | solution.py:202
  144.2 3.9 %copy-start.7 = (f32[1176,256]{1,0:T(8,128)S(1)}, f32[1176,256]{1,0:T(8,128)}, u32[]{:S(2)}) copy-start(f32[1176,256]{1,0:T(8,128)} %get-tuple-element.57) | copy-start | bytes 3612676
  147.1 28.9 %collective-permute-start.4 = (f32[1176,256]{1,0:T(8,128)}, f32[1176,256]{1,0:T(8,128)}, u32[]{:S(2)}, u32[]{:S(2)}) collective-permute-start(f32[1176,256]{1,0:T(8,128)} %add.98), channel_id=1, source_target_pairs={{0,2},{2,4},{4,6},{6,8},{8,10},{10,12},{12,14},{14,0},{1,3},{3,5},... | collective-permute-start | bytes 3612680 | tf_op jit(solution)/shard_map/ppermute | solution.py:220
  149.2 30.9 %collective-permute-start.7 = (f32[1176,256]{1,0:T(8,128)}, f32[1176,256]{1,0:T(8,128)S(1)}, u32[]{:S(2)}, u32[]{:S(2)}) collective-permute-start(f32[1176,256]{1,0:T(8,128)} %add.101), channel_id=1, source_target_pairs={{0,14},{2,0},{4,2},{6,4},{8,6},{10,8},{12,10},{14,12},{1,15},{3,1}... | collective-permute-start | bytes 3612680 | tf_op jit(solution)/shard_map/ppermute | solution.py:221
  161.4 1.4 copy-start.5
  176.0 4.1 %copy-start.8 = (f32[1176,256]{1,0:T(8,128)S(1)}, f32[1176,256]{1,0:T(8,128)}, u32[]{:S(2)}) copy-start(f32[1176,256]{1,0:T(8,128)} %get-tuple-element.58) | copy-start | bytes 3612676
  177.9 32.6 %collective-permute-start.5 = (f32[1176,256]{1,0:T(8,128)S(1)}, f32[1176,256]{1,0:T(8,128)S(1)}, u32[]{:S(2)}, u32[]{:S(2)}) collective-permute-start(f32[1176,256]{1,0:T(8,128)S(1)} %add.99), channel_id=1, source_target_pairs={{0,2},{2,4},{4,6},{6,8},{8,10},{10,12},{12,14},{14,0},{1,3},{3,5},... | collective-permute-start | bytes 3612680 | tf_op jit(solution)/shard_map/ppermute | solution.py:231
  180.1 1.2 copy-start.4
  180.3 30.2 %collective-permute-start.8 = (f32[1176,256]{1,0:T(8,128)S(1)}, f32[1176,256]{1,0:T(8,128)S(1)}, u32[]{:S(2)}, u32[]{:S(2)}) collective-permute-start(f32[1176,256]{1,0:T(8,128)S(1)} %add.102), channel_id=1, source_target_pairs={{0,14},{2,0},{4,2},{6,4},{8,6},{10,8},{12,10},{14,12},{1,15},{3,1}... | collective-permute-start | bytes 3612680 | tf_op jit(solution)/shard_map/ppermute | solution.py:232
where the time goes:
time: 240 us; the launch traced here: 236 us
  waiting for transfers between devices  70.3 us (29%)
  Pallas kernels  60.9 us (25%)
  blocking collectives  44.7 us (19%)
  starting transfers between devices  39.4 us (16%)
  local copies, waits for them, and re-layouts  12 us (5%)
  other arithmetic  8.75 us (4%)
    all_to_all x4, waiting for transfers between devices, swap(): got = lax.all_to_all(sent, PLANE, split_axis=0, concat_axis=0, tiled=True)  64.7 us
    pallas_call x4, Pallas kernels, contract(): pl.pallas_call(lambda *refs: product_kernel(n, *refs), out_shape=[jax.Sha...  34 us
    all_to_all x4, starting transfers between devices, swap(): got = lax.all_to_all(sent, PLANE, split_axis=0, concat_axis=0, tiled=True)  29.8 us
    all_to_all x1, blocking collectives, swap(): got = lax.all_to_all(sent, PLANE, split_axis=0, concat_axis=0, tiled=True)  22.5 us
    all_to_all x1, blocking collectives, on_device(): lax.all_to_all(total, ('x', 'yh'), split_axis=0, concat_axis=0, tiled=True)  22.2 us
    pallas_call x5, Pallas kernels, pack(): pl.pallas_call(lambda *refs: pack_kernel(n, *refs), out_shape=jax.ShapeDt...  15.3 us
    unnamed x26, local copies, waits for them, and re-layouts  9.57 us
    ppermute x4, starting transfers between devices, on_device(): right = lax.ppermute(right, 'z', up)  7.31 us
  transfers between devices with their start and end apart: 13, of which 6 were waited for; matrix products, arithmetic and copies ran while one was open for 3% of the time, Pallas kernels for 24%

commit v1 on v0

--- a/solution.py
+++ b/solution.py
@@ -63,31 +63,6 @@
     return out.reshape(32, rows, width)
 
 
-def prepare_kernel(in_ref, high_ref, low_ref):
-    value = (0.5 * in_ref[...]).T
-    high = value.astype(jnp.bfloat16)
-    high_ref[...] = high
-    low_ref[...] = (value - high.astype(jnp.float32)).astype(jnp.bfloat16)
-
-
-def prepare(slab, first):
-    depth = slab.shape[0]
-    half = jax.ShapeDtypeStruct((HALF, depth), jnp.bfloat16)
-    spec = pl.BlockSpec((128, depth), lambda k: (k, 0))
-    return pl.pallas_call(
-        prepare_kernel,
-        out_shape=(half, half),
-        grid=(HALF // 128,),
-        in_specs=[pl.BlockSpec((depth, 128), lambda k: (0, first + k))],
-        out_specs=(spec, spec),
-        compiler_params=SMALL,
-        cost_estimate=pl.CostEstimate(
-            flops=0, bytes_accessed=depth * HALF * 8, transcendentals=0
-        ),
-        name="prepare",
-    )(slab)
-
-
 def first_kernel(amps_ref, v_ref, out_ref):
     def split(value):
         high = value.astype(jnp.bfloat16)
@@ -127,68 +102,14 @@
     )(amps, slab)
 
 
-def product_kernel(n, core_ref, ha_ref, la_ref, hb_ref, lb_ref, v_ref, *refs):
-    outs, sums = refs[-2 - n : -2], refs[: -2 - n]
-    vh, vl = refs[-2:]
-    step = pl.program_id(0)
-
-    @pl.when(step == 0)
-    def _():
-        piece = v_ref[...]
-        high = piece.astype(jnp.bfloat16)
-        vh[...] = high
-        vl[...] = (piece - high.astype(jnp.float32)).astype(jnp.bfloat16)
-
-    def dot(left_side, right_side):
-        return jnp.dot(left_side, right_side, preferred_element_type=jnp.float32)
-
-    def rows(h_ref, l_ref, gets_sum):
-        value = dot(l_ref[...], vh[...]) + dot(h_ref[...], vl[...])
-        value += dot(h_ref[...], vh[...])
-        for k in range(n):
-            block = value[:, k * 256 : (k + 1) * 256]
-            outs[k][...] = block + sums[k][...] if sums and k == gets_sum else block
-
-    pl.when(step < 2)(lambda: rows(ha_ref, la_ref, 0))
-    pl.when(step >= 2)(lambda: rows(hb_ref, lb_ref, 1))
-
-
-def contract(core, amps, slab, n, sums=()):
-    depth = slab.shape[0]
-
-    def own(m):
-        return jnp.minimum(m, 1)
-
-    def other(m):
-        return jnp.maximum(m - 2, 0)
-
-    def place(m, core):
-        return jnp.where(m < 2, core[0] * 2 + m, (1 - core[0]) * 2 + m - 2), 0
-
-    return pl.pallas_call(
-        lambda *refs: product_kernel(n, *refs),
-        out_shape=[jax.ShapeDtypeStruct((IJ, 256), jnp.float32)] * n,
-        grid_spec=pltpu.PrefetchScalarGridSpec(
-            num_scalar_prefetch=1,
-            grid=(4,),
-            in_specs=[pl.BlockSpec((320, depth), lambda m, c: (own(m), 0))] * 2
-            + [pl.BlockSpec((320, depth), lambda m, c: (other(m), 0))] * 2
-            + [pl.BlockSpec((depth, n * 256), lambda m, c: (0, 0))]
-            + [
-                pl.BlockSpec((320, 256), lambda m, c: (own(m), 0)),
-                pl.BlockSpec((320, 256), lambda m, c: (other(m), 0)),
-            ][: len(sums)],
-            out_specs=[pl.BlockSpec((320, 256), place)] * n,
-            scratch_shapes=[pltpu.VMEM((depth, n * 256), jnp.bfloat16)] * 2,
-        ),
-        compiler_params=BIG,
-        cost_estimate=pl.CostEstimate(
-            flops=6 * n * IJ * depth * 256,
-            bytes_accessed=8 * depth * HALF + n * (depth + IJ) * 1024,
-            transcendentals=0,
-        ),
-        name="product",
-    )(core, *amps, slab, *sums)
+def contract(left_side, right_side):
+    return lax.dot_general(
+        left_side,
+        right_side,
+        (((0,), (0,)), ((), ())),
+        precision=lax.Precision.HIGH,
+        preferred_element_type=jnp.float32,
+    )
 
 
 def on_device(amplitudes, integrals):
@@ -212,26 +133,31 @@
     width = len(CHUNKS[0]) * 256
     own = slab[:, width:]
     other = lax.ppermute(own, "c", [(0, 1), (1, 0)])
-    right, left = first(own, slab), first(other, slab)
+    is_first = core[0] == 0
+
+    def in_order(one, two, axis):
+        return (
+            jnp.where(is_first, one, two),
+            lax.slice_in_dim(jnp.where(is_first, two, one), 0, IJ - HALF, axis=axis),
+        )
+
+    right, left = in_order(first(own, slab), first(other, slab), 0)
     own, other, right, left = lax.optimization_barrier((own, other, right, left))
-    amps = (*prepare(own, 0), *prepare(other, 0))
+    amps = 0.5 * jnp.concatenate(in_order(own, other, 1), axis=1)
 
     for place in range(1, 4):
         right = lax.ppermute(right, "z", up)
         left = lax.ppermute(left, "z", down)
         slab = swap(sent[place])
         if place == 1:
-            right, left, slab, sent[2], *amps = lax.optimization_barrier(
-                (right, left, slab, sent[2], *amps)
-            )
-            right, left = contract(core, amps, slab, 2, (right, left))
-            continue
-        ups, downs = contract(core, amps, slab, 2)
-        right, left = right + ups, left + downs
+            right, left, slab, amps = lax.optimization_barrier((right, left, slab, amps))
+            right = jnp.pad(right, ((0, IJ - HALF), (0, 0)))
+            left = jnp.pad(left, ((HALF, 0), (0, 0)))
+        product = lax.optimization_barrier(contract(amps, slab))
+        right, left = right + product[:, :256], left + product[:, 256:]
     right = lax.ppermute(right, "z", up)
     left = lax.ppermute(left, "z", down)
-    own = contract(core, amps, swap(sent[4]), 1)[0]
-    total = (own + right + left).reshape(8, ROWS, 256)
+    total = (contract(amps, swap(sent[4])) + right + left).reshape(8, ROWS, 256)
     got = lax.all_to_all(total, ("x", "yh"), split_axis=0, concat_axis=0, tiled=True)
     return got.transpose(1, 0, 2).reshape(ROWS, 8 * 256)
 

time: 240 us -> 237 us (0.988)
  Pallas kernels: 60.9 us -> 21 us
  matrix products: 0 us -> 26.7 us
  waiting for transfers between devices: 70.3 us -> 80.7 us
  other arithmetic: 8.75 us -> 17.7 us
  local copies, waits for them, and re-layouts: 12 us -> 4.04 us
    pallas_call x6 -> x0, Pallas kernels: 39 us -> none  [the longest x4 34 us: contract(): pl.pallas_call(lambda *refs: product_kernel(n, *refs), out_shape=[jax.Sha...]
    dot_general x0 -> x4, matrix products: none -> 26.7 us  [contract(): lax.dot_general(left_side, right_side, (((0,), (0,)), ((), ())), precisio...]
    ppermute x4, waiting for transfers between devices: 4.19 us -> 13.6 us  [on_device(): right = lax.ppermute(right, 'z', up)]
    unnamed x26 -> x18, local copies, waits for them, and re-layouts: 9.57 us -> 1.59 us
    select_n x0 -> x4, other arithmetic: none -> 7.15 us  [the longest x2 4.41 us: in_order(): jnp.where(is_first, two, one)]
    ppermute x4, waiting for transfers between devices: 1.38 us -> 6.34 us  [on_device(): left = lax.ppermute(left, 'z', down)]
    all_to_all x4, waiting for transfers between devices: 64.7 us -> 60.7 us  [swap(): got = lax.all_to_all(sent, PLANE, split_axis=0, concat_axis=0, tiled=True)]
    add x5 -> x3, other arithmetic: 7.65 us -> 7.33 us  [on_device(): right, left = (right + product[:, :256], left + product[:, 256:])]
  transfers between devices with their start and end apart: 13 -> 13, of which waited for: 6 -> 10; matrix products, arithmetic and copies ran while one was open for 3% -> 16% of each run, Pallas kernels for 24% -> 8%
where the time goes in v1:
time: 237 us; the launch traced here: 234 us
  waiting for transfers between devices  80.7 us (34%)
  blocking collectives  43.7 us (18%)
  starting transfers between devices  40.3 us (17%)
  matrix products  26.7 us (11%)
  Pallas kernels  21 us (9%)
  other arithmetic  17.7 us (7%)
  local copies, waits for them, and re-layouts  4.04 us (2%)
    all_to_all x4, waiting for transfers between devices, swap(): got = lax.all_to_all(sent, PLANE, split_axis=0, concat_axis=0, tiled=True)  60.7 us
    all_to_all x4, starting transfers between devices, swap(): got = lax.all_to_all(sent, PLANE, split_axis=0, concat_axis=0, tiled=True)  29.7 us
    dot_general x4, matrix products, contract(): lax.dot_general(left_side, right_side, (((0,), (0,)), ((), ())), precisio...  26.7 us
    all_to_all x1, blocking collectives, swap(): got = lax.all_to_all(sent, PLANE, split_axis=0, concat_axis=0, tiled=True)  22.4 us
    all_to_all x1, blocking collectives, on_device(): lax.all_to_all(total, ('x', 'yh'), split_axis=0, concat_axis=0, tiled=True)  21.3 us
    pallas_call x5, Pallas kernels, pack(): pl.pallas_call(lambda *refs: pack_kernel(n, *refs), out_shape=jax.ShapeDt...  15.3 us
    ppermute x4, waiting for transfers between devices, on_device(): right = lax.ppermute(right, 'z', up)  13.6 us
    add x3, other arithmetic, on_device(): right, left = (right + product[:, :256], left + product[:, 256:])  7.33 us
  transfers between devices with their start and end apart: 13, of which 10 were waited for; matrix products, arithmetic and copies ran while one was open for 16% of the time, Pallas kernels for 8%

profile of v1, /device:TPU:102, one launch (start us, length us, event | category | flops | bytes accessed | tf_op | source)
XLA Modules:
  0.0 234.4 jit_solution(18295755779457850240)
XLA Ops:
  0.0 3.0 %pack.5 = f32[8,4,32,896]{3,2,1,0:T(8,128)} custom-call(s32[1]{0:T(128)S(6)} %select_n.49.refs_0_, f32[32,65536]{1,0:T(8,128)} %refs_1_.9, f32[32,1176]{1,0:T(8,128)} %refs_2_.4), custom_call_target="tpu_custom_call" | custom-call | bytes 7340032 | tf_op jit(solution)/shard_map/pack/pallas_call | solution.py:47
  3.0 7.7 %all-to-all-start = ((f32[32,32,896]{2,1,0:T(8,128)}), f32[32,32,896]{2,1,0:T(8,128)}, u32[]{:S(2)}, u32[]{:S(2)}) async-start(f32[32,32,896]{2,1,0:T(8,128)} %bitcast.26), calls=%async_computation | async-start | bytes 7340032 | tf_op jit(solution)/shard_map/all_to_all | solution.py:123
  10.7 2.1 pack.9
  12.8 0.6 and_select_fusion
  13.4 3.4 %pack.8 = f32[8,4,32,512]{3,2,1,0:T(8,128)} custom-call(s32[2]{0:T(128)} %get-tuple-element.37.refs_0_, f32[32,65536]{1,0:T(8,128)} %refs_1_.9, f32[32,65536]{1,0:T(8,128)} %refs_1_.9), custom_call_target="tpu_custom_call" | custom-call | bytes 4194304 | tf_op jit(solution)/shard_map/pack/pallas_call | solution.py:47
  16.8 0.5 and_select_fusion.2.refs_0_
  17.4 3.3 %pack.6 = f32[8,4,32,512]{3,2,1,0:T(8,128)} custom-call(s32[2]{0:T(128)} %and_select_fusion.2.refs_0_, f32[32,65536]{1,0:T(8,128)} %refs_1_.9, f32[32,65536]{1,0:T(8,128)} %refs_1_.9), custom_call_target="tpu_custom_call" | custom-call | bytes 4194304 | tf_op jit(solution)/shard_map/pack/pallas_call | solution.py:47
  20.7 3.4 %pack.7 = f32[8,4,32,512]{3,2,1,0:T(8,128)} custom-call(s32[2]{0:T(128)} %get-tuple-element.38.refs_0_, f32[32,65536]{1,0:T(8,128)} %refs_1_.9, f32[32,65536]{1,0:T(8,128)} %refs_1_.9), custom_call_target="tpu_custom_call" | custom-call | bytes 4194304 | tf_op jit(solution)/shard_map/pack/pallas_call | solution.py:47
  24.1 31.4 %all-to-all-done = f32[32,32,896]{2,1,0:T(8,128)} async-done(((f32[32,32,896]{2,1,0:T(8,128)}), f32[32,32,896]{2,1,0:T(8,128)}, u32[]{:S(2)}, u32[]{:S(2)}) %all-to-all-start) | async-done | bytes 3670048 | tf_op jit(solution)/shard_map/all_to_all | solution.py:123
  55.4 1.9 slice.27.amps_ref
  57.4 8.2 %all-to-all-start.1 = ((f32[32,32,512]{2,1,0:T(8,128)}), f32[32,32,512]{2,1,0:T(8,128)}, u32[]{:S(2)}, u32[]{:S(2)}) async-start(f32[32,32,512]{2,1,0:T(8,128)} %bitcast.30), calls=%async_computation.1 | async-start | bytes 4194304 | tf_op jit(solution)/shard_map/all_to_all | solution.py:123
  65.6 2.5 %first.2 = f32[640,256]{1,0:T(8,128)S(1)} custom-call(f32[1024,640]{1,0:T(8,128)S(1)} %slice.27.amps_ref, f32[1024,896]{1,0:T(8,128)} %bitcast.2.v_ref), custom_call_target="tpu_custom_call" | custom-call | flops 1006632960 | bytes 4325376 | tf_op jit(solution)/shard_map/first/pallas_call | solution.py:86
  68.1 3.3 %first.3 = f32[640,256]{1,0:T(8,128)S(1)} custom-call(f32[1024,640]{1,0:T(8,128)} %collective-permute-done.amps_ref, f32[1024,896]{1,0:T(8,128)} %bitcast.2.v_ref), custom_call_target="tpu_custom_call" | custom-call | flops 1006632960 | bytes 4325376 | tf_op jit(solution)/shard_map/first/pallas_call | solution.py:86
  71.4 0.9 slice_select_fusion.1
  72.3 0.9 broadcast_select_fusion.1
  73.2 0.1 collective-permute-start.2
  73.3 3.1 %collective-permute-start.1 = (f32[640,256]{1,0:T(8,128)}, f32[640,256]{1,0:T(8,128)S(1)}, u32[]{:S(2)}, u32[]{:S(2)}) collective-permute-start(f32[640,256]{1,0:T(8,128)} %broadcast_select_fusion.1), channel_id=1, source_target_pairs={{0,2},{2,4},{4,6},{6,8},{8,10},{10,12},{12,14},{14,0},{1,3},{3,5},... | collective-permute-start | bytes 1966088 | tf_op jit(solution)/shard_map/ppermute | solution.py:149
  76.4 3.5 %slice_select_fusion = f32[1024,536]{1,0:T(8,128)} fusion(f32[1024,640]{1,0:T(8,128)S(1)} %slice.27.amps_ref, f32[1024,640]{1,0:T(8,128)} %collective-permute-done.amps_ref, pred[]{:T(512)S(6)} %eq.10), kind=kLoop, calls=%fused_computation.3 | loop fusion | flops 548864 | bytes 6586369 | tf_op jit(solution)/shard_map/jit(_where)/select_n | solution.py:141
  79.9 1.8 broadcast_select_fusion
  81.8 10.2 %all-to-all-done.1 = f32[32,32,512]{2,1,0:T(8,128)} async-done(((f32[32,32,512]{2,1,0:T(8,128)}), f32[32,32,512]{2,1,0:T(8,128)}, u32[]{:S(2)}, u32[]{:S(2)}) %all-to-all-start.1) | async-done | bytes 2097184 | tf_op jit(solution)/shard_map/all_to_all | solution.py:123
  92.0 7.3 %all-to-all-start.3 = ((f32[32,32,512]{2,1,0:T(8,128)}), f32[32,32,512]{2,1,0:T(8,128)}, u32[]{:S(2)}, u32[]{:S(2)}) async-start(f32[32,32,512]{2,1,0:T(8,128)} %bitcast.29), calls=%async_computation.3 | async-start | bytes 4194304 | tf_op jit(solution)/shard_map/all_to_all | solution.py:123
  99.3 2.1 maximum_multiply_fusion
  101.5 7.8 %fusion.4 = f32[1176,512]{1,0:T(8,128)S(1)} fusion(f32[1024,1176]{1,0:T(8,128)S(1)} %maximum_multiply_fusion, f32[1024,512]{1,0:T(8,128)} %bitcast.8), kind=kOutput, calls=%fused_computation.25 | convolution fusion | flops 3699376128 | bytes 9322496 | tf_op jit(solution)/shard_map/dot_general | solution.py:106
  109.3 2.7 %slice_add_fusion.5 = (f32[1176,256]{1,0:T(8,128)}, f32[1176,256]{1,0:T(8,128)}) fusion(f32[1176,512]{1,0:T(8,128)S(1)} %fusion.4, f32[640,256]{1,0:T(8,128)S(1)} %collective-permute-done.1, f32[536,256]{1,0:T(8,128)} %collective-permute-done.2), kind=kLoop, calls=%fused_computation.10 | loop fusion | flops 602112 | bytes 6021120 | tf_op jit(solution)/shard_map/add | solution.py:157
  112.0 3.1 %collective-permute-start.3 = (f32[1176,256]{1,0:T(8,128)}, f32[1176,256]{1,0:T(8,128)S(1)}, u32[]{:S(2)}, u32[]{:S(2)}) collective-permute-start(f32[1176,256]{1,0:T(8,128)} %get-tuple-element.35), channel_id=1, source_target_pairs={{0,2},{2,4},{4,6},{6,8},{8,10},{10,12},{12,14},{14,0},{1,3},{3,5},... | collective-permute-start | bytes 3612680 | tf_op jit(solution)/shard_map/ppermute | solution.py:149
  115.1 10.5 %all-to-all-done.3 = f32[32,32,512]{2,1,0:T(8,128)} async-done(((f32[32,32,512]{2,1,0:T(8,128)}), f32[32,32,512]{2,1,0:T(8,128)}, u32[]{:S(2)}, u32[]{:S(2)}) %all-to-all-start.3) | async-done | bytes 2097184 | tf_op jit(solution)/shard_map/all_to_all | solution.py:123
  125.7 6.6 %all-to-all-start.4 = ((f32[32,32,512]{2,1,0:T(8,128)}), f32[32,32,512]{2,1,0:T(8,128)S(1)}, u32[]{:S(2)}, u32[]{:S(2)}) async-start(f32[32,32,512]{2,1,0:T(8,128)} %bitcast.28), calls=%async_computation.4 | async-start | bytes 4194304 | tf_op jit(solution)/shard_map/all_to_all | solution.py:123
  132.3 7.6 %fusion.5 = f32[1176,512]{1,0:T(8,128)S(1)} fusion(f32[1024,1176]{1,0:T(8,128)} %copy-done, f32[1024,512]{1,0:T(8,128)} %bitcast.10), kind=kOutput, calls=%fused_computation.26 | convolution fusion | flops 3699376128 | bytes 9322496 | tf_op jit(solution)/shard_map/dot_general | solution.py:106
  139.9 1.6 collective-permute-done.3
  141.5 3.4 %collective-permute-done.6 = f32[1176,256]{1,0:T(8,128)} collective-permute-done((f32[1176,256]{1,0:T(8,128)}, f32[1176,256]{1,0:T(8,128)}, u32[]{:S(2)}, u32[]{:S(2)}) %collective-permute-start.6) | collective-permute-done | bytes 1204256 | tf_op jit(solution)/shard_map/ppermute | solution.py:150
  144.9 3.0 %slice_add_fusion.4 = (f32[1176,256]{1,0:T(8,128)}, f32[1176,256]{1,0:T(8,128)}) fusion(f32[1176,256]{1,0:T(8,128)S(1)} %collective-permute-done.3, f32[1176,512]{1,0:T(8,128)S(1)} %fusion.5, f32[1176,256]{1,0:T(8,128)} %collective-permute-done.6), kind=kLoop, calls=%fused_computation.9 | loop fusion | flops 602112 | bytes 7225344 | tf_op jit(solution)/shard_map/add | solution.py:157
  148.0 0.2 collective-permute-start.4
  148.1 1.8 collective-permute-start.7
  150.0 8.6 %all-to-all-done.4 = f32[32,32,512]{2,1,0:T(8,128)S(1)} async-done(((f32[32,32,512]{2,1,0:T(8,128)}), f32[32,32,512]{2,1,0:T(8,128)S(1)}, u32[]{:S(2)}, u32[]{:S(2)}) %all-to-all-start.4) | async-done | bytes 2097184 | tf_op jit(solution)/shard_map/all_to_all | solution.py:123
  158.6 7.1 %fusion.6 = f32[1176,512]{1,0:T(8,128)S(1)} fusion(f32[1024,1176]{1,0:T(8,128)} %copy-done, f32[1024,512]{1,0:T(8,128)S(1)} %bitcast.27), kind=kOutput, calls=%fused_computation.27 | convolution fusion | flops 3699376128 | bytes 9322496 | tf_op jit(solution)/shard_map/dot_general | solution.py:106
  165.7 9.9 %collective-permute-done.4 = f32[1176,256]{1,0:T(8,128)S(1)} collective-permute-done((f32[1176,256]{1,0:T(8,128)}, f32[1176,256]{1,0:T(8,128)S(1)}, u32[]{:S(2)}, u32[]{:S(2)}) %collective-permute-start.4) | collective-permute-done | bytes 1204256 | tf_op jit(solution)/shard_map/ppermute | solution.py:149
  175.6 1.5 collective-permute-done.7
  177.1 1.6 slice_add_fusion.3
  178.7 0.3 collective-permute-start.5
  179.0 1.8 collective-permute-start.8
  180.8 22.4 %all_to_all.30 = f32[32,32,256]{2,1,0:T(8,128)S(1)} all-to-all(f32[32,32,256]{2,1,0:T(8,128)S(1)} %bitcast.33), channel_id=1, replica_groups=mesh['x'=4,'yh'=2,'yl'=2,'z'=8,'c'=2] {'x','yh','yl','c'}, dimensions={0} | all-to-all | bytes 2097152 | tf_op jit(solution)/shard_map/all_to_all | solution.py:123
  203.3 2.1 collective-permute-done.5
  205.3 1.4 collective-permute-done.8
  206.7 4.3 %fusion = f32[1176,256]{1,0:T(8,128)S(1)} fusion(f32[1176,256]{1,0:T(8,128)S(1)} %collective-permute-done.8, f32[1176,256]{1,0:T(8,128)S(1)} %collective-permute-done.5, f32[1024,1176]{1,0:T(8,128)S(1)} %bitcast.25, f32[1024,256]{1,0:T(8,128)S(1)} %bitcast.34), kind=kOutput, calls=%fused_computation.2 | convolution fusion | flops 1850290176 | bytes 9478144 | tf_op jit(solution)/shard_map/dot_general | solution.py:106
  211.0 0.1 reshape.50
  211.2 21.3 %all_to_all.31 = f32[8,147,256]{2,1,0:T(8,128)S(1)} all-to-all(f32[8,147,256]{2,1,0:T(8,128)S(1)} %reshape.50), channel_id=1, replica_groups=mesh['x'=4,'yh'=2,'yl'=2,'z'=8,'c'=2] {'x','yh'}, dimensions={0} | all-to-all | bytes 2408448 | tf_op jit(solution)/shard_map/all_to_all | solution.py:161
  232.5 0.4 copy.9
  232.9 1.5 copy.10
  (23 shorter events, 0.2 us)
Async XLA Ops:
  3.0 52.4 %all-to-all-start = ((f32[32,32,896]{2,1,0:T(8,128)}), f32[32,32,896]{2,1,0:T(8,128)}, u32[]{:S(2)}, u32[]{:S(2)}) async-start(f32[32,32,896]{2,1,0:T(8,128)} %bitcast.26), calls=%async_computation | async-start | bytes 7340032 | tf_op jit(solution)/shard_map/all_to_all | solution.py:123
  10.7 2.1 copy-start.3
  10.7 2.1 copy-start.4
  13.4 3.5 %copy-start.5 = (s32[2]{0:T(128)S(1)}, s32[2]{0:T(128)}, u32[]{:S(2)}) copy-start(s32[2]{0:T(128)} %constant.73.clone) | copy-start | bytes 28
  57.3 10.8 %collective-permute-start = (f32[1024,640]{1,0:T(8,128)S(1)}, f32[1024,640]{1,0:T(8,128)}, u32[]{:S(2)}, u32[]{:S(2)}) collective-permute-start(f32[1024,640]{1,0:T(8,128)S(1)} %slice.27.amps_ref), channel_id=1, source_target_pairs={{0,1},{1,0},{2,3},{3,2},{4,5},{5,4},{6,7},{7,6},{8,9},{9,8},{10,11... | collective-permute-start | bytes 7864328 | tf_op jit(solution)/shard_map/ppermute | solution.py:135
  57.4 34.6 %all-to-all-start.1 = ((f32[32,32,512]{2,1,0:T(8,128)}), f32[32,32,512]{2,1,0:T(8,128)}, u32[]{:S(2)}, u32[]{:S(2)}) async-start(f32[32,32,512]{2,1,0:T(8,128)} %bitcast.30), calls=%async_computation.1 | async-start | bytes 4194304 | tf_op jit(solution)/shard_map/all_to_all | solution.py:123
  73.2 28.3 %collective-permute-start.2 = (f32[536,256]{1,0:T(8,128)}, f32[536,256]{1,0:T(8,128)}, u32[]{:S(2)}, u32[]{:S(2)}) collective-permute-start(f32[536,256]{1,0:T(8,128)} %slice_select_fusion.1), channel_id=1, source_target_pairs={{0,14},{2,0},{4,2},{6,4},{8,6},{10,8},{12,10},{14,12},{1,15},{3,1}... | collective-permute-start | bytes 1646600 | tf_op jit(solution)/shard_map/ppermute | solution.py:150
  73.3 28.2 %collective-permute-start.1 = (f32[640,256]{1,0:T(8,128)}, f32[640,256]{1,0:T(8,128)S(1)}, u32[]{:S(2)}, u32[]{:S(2)}) collective-permute-start(f32[640,256]{1,0:T(8,128)} %broadcast_select_fusion.1), channel_id=1, source_target_pairs={{0,2},{2,4},{4,6},{6,8},{8,10},{10,12},{12,14},{14,0},{1,3},{3,5},... | collective-permute-start | bytes 1966088 | tf_op jit(solution)/shard_map/ppermute | solution.py:149
  81.8 17.5 %copy-start.1 = (f32[1024,536]{1,0:T(8,128)S(1)}, f32[1024,536]{1,0:T(8,128)}, u32[]{:S(2)}) copy-start(f32[1024,536]{1,0:T(8,128)} %slice_select_fusion) | copy-start | bytes 6586372
  92.0 33.7 %all-to-all-start.3 = ((f32[32,32,512]{2,1,0:T(8,128)}), f32[32,32,512]{2,1,0:T(8,128)}, u32[]{:S(2)}, u32[]{:S(2)}) async-start(f32[32,32,512]{2,1,0:T(8,128)} %bitcast.29), calls=%async_computation.3 | async-start | bytes 4194304 | tf_op jit(solution)/shard_map/all_to_all | solution.py:123
  101.5 7.8 %copy-start = (f32[1024,1176]{1,0:T(8,128)}, f32[1024,1176]{1,0:T(8,128)S(1)}, u32[]{:S(2)}) copy-start(f32[1024,1176]{1,0:T(8,128)S(1)} %maximum_multiply_fusion) | copy-start | bytes 14450692
  112.0 29.5 %collective-permute-start.3 = (f32[1176,256]{1,0:T(8,128)}, f32[1176,256]{1,0:T(8,128)S(1)}, u32[]{:S(2)}, u32[]{:S(2)}) collective-permute-start(f32[1176,256]{1,0:T(8,128)} %get-tuple-element.35), channel_id=1, source_target_pairs={{0,2},{2,4},{4,6},{6,8},{8,10},{10,12},{12,14},{14,0},{1,3},{3,5},... | collective-permute-start | bytes 3612680 | tf_op jit(solution)/shard_map/ppermute | solution.py:149
  115.1 29.8 %collective-permute-start.6 = (f32[1176,256]{1,0:T(8,128)}, f32[1176,256]{1,0:T(8,128)}, u32[]{:S(2)}, u32[]{:S(2)}) collective-permute-start(f32[1176,256]{1,0:T(8,128)} %get-tuple-element.36), channel_id=1, source_target_pairs={{0,14},{2,0},{4,2},{6,4},{8,6},{10,8},{12,10},{14,12},{1,15},{3,1}... | collective-permute-start | bytes 3612680 | tf_op jit(solution)/shard_map/ppermute | solution.py:150
  125.7 32.9 %all-to-all-start.4 = ((f32[32,32,512]{2,1,0:T(8,128)}), f32[32,32,512]{2,1,0:T(8,128)S(1)}, u32[]{:S(2)}, u32[]{:S(2)}) async-start(f32[32,32,512]{2,1,0:T(8,128)} %bitcast.28), calls=%async_computation.4 | async-start | bytes 4194304 | tf_op jit(solution)/shard_map/all_to_all | solution.py:123
  148.0 27.6 %collective-permute-start.4 = (f32[1176,256]{1,0:T(8,128)}, f32[1176,256]{1,0:T(8,128)S(1)}, u32[]{:S(2)}, u32[]{:S(2)}) collective-permute-start(f32[1176,256]{1,0:T(8,128)} %get-tuple-element.33), channel_id=1, source_target_pairs={{0,2},{2,4},{4,6},{6,8},{8,10},{10,12},{12,14},{14,0},{1,3},{3,5},... | collective-permute-start | bytes 3612680 | tf_op jit(solution)/shard_map/ppermute | solution.py:149
  148.1 29.0 %collective-permute-start.7 = (f32[1176,256]{1,0:T(8,128)}, f32[1176,256]{1,0:T(8,128)}, u32[]{:S(2)}, u32[]{:S(2)}) collective-permute-start(f32[1176,256]{1,0:T(8,128)} %get-tuple-element.34), channel_id=1, source_target_pairs={{0,14},{2,0},{4,2},{6,4},{8,6},{10,8},{12,10},{14,12},{1,15},{3,1}... | collective-permute-start | bytes 3612680 | tf_op jit(solution)/shard_map/ppermute | solution.py:150
  158.6 48.1 %slice-start = ((s8[5242880]{0:T(1024)(128)(4,1)}), s8[4194304]{0:T(1024)(128)(4,1)S(1)}, s32[]{:S(2)}) async-start(s8[5242880]{0:T(1024)(128)(4,1)} %bitcast.24), calls=%async_computation.6 | async-start | bytes 8388608
  158.6 48.1 %slice-start.1 = ((s8[5242880]{0:T(1024)(128)(4,1)}), s8[1048576]{0:T(1024)(128)(4,1)S(1)}, s32[]{:S(2)}) async-start(s8[5242880]{0:T(1024)(128)(4,1)} %bitcast.24), calls=%async_computation.7 | async-start | bytes 2097152
  165.7 15.2 %copy-start.2 = (f32[8,4,32,256]{3,2,1,0:T(8,128)S(1)}, f32[8,4,32,256]{3,2,1,0:T(8,128)}, u32[]{:S(2)}) copy-start(f32[8,4,32,256]{3,2,1,0:T(8,128)} %pack.9) | copy-start | bytes 3145732
  178.7 26.6 %collective-permute-start.5 = (f32[1176,256]{1,0:T(8,128)S(1)}, f32[1176,256]{1,0:T(8,128)S(1)}, u32[]{:S(2)}, u32[]{:S(2)}) collective-permute-start(f32[1176,256]{1,0:T(8,128)S(1)} %get-tuple-element.31), channel_id=1, source_target_pairs={{0,2},{2,4},{4,6},{6,8},{8,10},{10,12},{12,14},{14,0},{1,3},{3,5},... | collective-permute-start | bytes 3612680 | tf_op jit(solution)/shard_map/ppermute | solution.py:158
  179.0 27.7 %collective-permute-start.8 = (f32[1176,256]{1,0:T(8,128)S(1)}, f32[1176,256]{1,0:T(8,128)S(1)}, u32[]{:S(2)}, u32[]{:S(2)}) collective-permute-start(f32[1176,256]{1,0:T(8,128)S(1)} %get-tuple-element.32), channel_id=1, source_target_pairs={{0,14},{2,0},{4,2},{6,4},{8,6},{10,8},{12,10},{14,12},{1,15},{3,1}... | collective-permute-start | bytes 3612680 | tf_op jit(solution)/shard_map/ppermute | solution.py:159

commit v2 on v1

--- a/solution.py
+++ b/solution.py
@@ -144,6 +144,7 @@
     right, left = in_order(first(own, slab), first(other, slab), 0)
     own, other, right, left = lax.optimization_barrier((own, other, right, left))
     amps = 0.5 * jnp.concatenate(in_order(own, other, 1), axis=1)
+    amps, sent[2] = lax.optimization_barrier((amps, sent[2]))
 
     for place in range(1, 4):
         right = lax.ppermute(right, "z", up)

time: 237 us -> 237 us (level)
  other arithmetic: 17.7 us -> 15 us
    all_to_all x4, waiting for transfers between devices: 60.7 us -> 66.7 us  [swap(): got = lax.all_to_all(sent, PLANE, split_axis=0, concat_axis=0, tiled=True)]
    ppermute x4, waiting for transfers between devices: 13.6 us -> 8.73 us  [on_device(): right = lax.ppermute(right, 'z', up)]
  transfers between devices with their start and end apart: 13 -> 13, of which waited for: 10 -> 9; matrix products, arithmetic and copies ran while one was open for 16% -> 15% of each run, Pallas kernels for 8% -> 8%
where the time goes in v2:
time: 237 us; the launch traced here: 234 us
  waiting for transfers between devices  82.2 us (35%)
  blocking collectives  44.7 us (19%)
  starting transfers between devices  40.3 us (17%)
  matrix products  26.5 us (11%)
  Pallas kernels  21 us (9%)
  other arithmetic  15 us (6%)
  local copies, waits for them, and re-layouts  4.03 us (2%)
    all_to_all x4, waiting for transfers between devices, swap(): got = lax.all_to_all(sent, PLANE, split_axis=0, concat_axis=0, tiled=True)  66.7 us
    all_to_all x4, starting transfers between devices, swap(): got = lax.all_to_all(sent, PLANE, split_axis=0, concat_axis=0, tiled=True)  29.7 us
    dot_general x4, matrix products, contract(): lax.dot_general(left_side, right_side, (((0,), (0,)), ((), ())), precisio...  26.5 us
    all_to_all x1, blocking collectives, swap(): got = lax.all_to_all(sent, PLANE, split_axis=0, concat_axis=0, tiled=True)  22.4 us
    all_to_all x1, blocking collectives, on_device(): lax.all_to_all(total, ('x', 'yh'), split_axis=0, concat_axis=0, tiled=True)  22.2 us
    pallas_call x5, Pallas kernels, pack(): pl.pallas_call(lambda *refs: pack_kernel(n, *refs), out_shape=jax.ShapeDt...  15.3 us
    ppermute x4, waiting for transfers between devices, on_device(): right = lax.ppermute(right, 'z', up)  8.73 us
    ppermute x4, starting transfers between devices, on_device(): right = lax.ppermute(right, 'z', up)  7.07 us
  transfers between devices with their start and end apart: 13, of which 9 were waited for; matrix products, arithmetic and copies ran while one was open for 15% of the time, Pallas kernels for 8%

profile of v2, /device:TPU:102, one launch (start us, length us, event | category | flops | bytes accessed | tf_op | source)
XLA Modules:
  0.0 233.8 jit_solution(17667401523870885381)
XLA Ops:
  0.0 3.0 %pack.5 = f32[8,4,32,896]{3,2,1,0:T(8,128)} custom-call(s32[1]{0:T(128)S(6)} %select_n.49.refs_0_, f32[32,65536]{1,0:T(8,128)} %refs_1_.9, f32[32,1176]{1,0:T(8,128)} %refs_2_.4), custom_call_target="tpu_custom_call" | custom-call | bytes 7340032 | tf_op jit(solution)/shard_map/pack/pallas_call | solution.py:47
  3.0 7.7 %all-to-all-start = ((f32[32,32,896]{2,1,0:T(8,128)}), f32[32,32,896]{2,1,0:T(8,128)}, u32[]{:S(2)}, u32[]{:S(2)}) async-start(f32[32,32,896]{2,1,0:T(8,128)} %bitcast.26), calls=%async_computation | async-start | bytes 7340032 | tf_op jit(solution)/shard_map/all_to_all | solution.py:123
  10.7 2.1 pack.9
  12.8 0.5 and_select_fusion
  13.4 3.5 %pack.8 = f32[8,4,32,512]{3,2,1,0:T(8,128)} custom-call(s32[2]{0:T(128)} %get-tuple-element.41.refs_0_, f32[32,65536]{1,0:T(8,128)} %refs_1_.9, f32[32,65536]{1,0:T(8,128)} %refs_1_.9), custom_call_target="tpu_custom_call" | custom-call | bytes 4194304 | tf_op jit(solution)/shard_map/pack/pallas_call | solution.py:47
  16.8 0.5 and_select_fusion.2.refs_0_
  17.3 3.4 %pack.6 = f32[8,4,32,512]{3,2,1,0:T(8,128)} custom-call(s32[2]{0:T(128)} %and_select_fusion.2.refs_0_, f32[32,65536]{1,0:T(8,128)} %refs_1_.9, f32[32,65536]{1,0:T(8,128)} %refs_1_.9), custom_call_target="tpu_custom_call" | custom-call | bytes 4194304 | tf_op jit(solution)/shard_map/pack/pallas_call | solution.py:47
  20.7 3.3 %pack.7 = f32[8,4,32,512]{3,2,1,0:T(8,128)} custom-call(s32[2]{0:T(128)} %get-tuple-element.42.refs_0_, f32[32,65536]{1,0:T(8,128)} %refs_1_.9, f32[32,65536]{1,0:T(8,128)} %refs_1_.9), custom_call_target="tpu_custom_call" | custom-call | bytes 4194304 | tf_op jit(solution)/shard_map/pack/pallas_call | solution.py:47
  24.0 31.4 %all-to-all-done = f32[32,32,896]{2,1,0:T(8,128)} async-done(((f32[32,32,896]{2,1,0:T(8,128)}), f32[32,32,896]{2,1,0:T(8,128)}, u32[]{:S(2)}, u32[]{:S(2)}) %all-to-all-start) | async-done | bytes 3670048 | tf_op jit(solution)/shard_map/all_to_all | solution.py:123
  55.4 1.9 slice.27.amps_ref
  57.3 0.1 collective-permute-start
  57.4 8.2 %all-to-all-start.1 = ((f32[32,32,512]{2,1,0:T(8,128)}), f32[32,32,512]{2,1,0:T(8,128)}, u32[]{:S(2)}, u32[]{:S(2)}) async-start(f32[32,32,512]{2,1,0:T(8,128)} %bitcast.30), calls=%async_computation.1 | async-start | bytes 4194304 | tf_op jit(solution)/shard_map/all_to_all | solution.py:123
  65.6 2.5 %first.2 = f32[640,256]{1,0:T(8,128)S(1)} custom-call(f32[1024,640]{1,0:T(8,128)S(1)} %slice.27.amps_ref, f32[1024,896]{1,0:T(8,128)} %bitcast.2.v_ref), custom_call_target="tpu_custom_call" | custom-call | flops 1006632960 | bytes 4325376 | tf_op jit(solution)/shard_map/first/pallas_call | solution.py:86
  68.1 3.3 %first.3 = f32[640,256]{1,0:T(8,128)S(1)} custom-call(f32[1024,640]{1,0:T(8,128)} %collective-permute-done.amps_ref, f32[1024,896]{1,0:T(8,128)} %bitcast.2.v_ref), custom_call_target="tpu_custom_call" | custom-call | flops 1006632960 | bytes 4325376 | tf_op jit(solution)/shard_map/first/pallas_call | solution.py:86
  71.4 0.9 slice_select_fusion.1
  72.3 0.9 broadcast_select_fusion.1
  73.2 0.1 collective-permute-start.2
  73.3 3.1 %collective-permute-start.1 = (f32[640,256]{1,0:T(8,128)}, f32[640,256]{1,0:T(8,128)S(1)}, u32[]{:S(2)}, u32[]{:S(2)}) collective-permute-start(f32[640,256]{1,0:T(8,128)} %broadcast_select_fusion.1), channel_id=1, source_target_pairs={{0,2},{2,4},{4,6},{6,8},{8,10},{10,12},{12,14},{14,0},{1,3},{3,5},... | collective-permute-start | bytes 1966088 | tf_op jit(solution)/shard_map/ppermute | solution.py:150
  76.4 2.0 slice_select_fusion
  78.5 0.3 broadcast_select_fusion
  78.8 2.7 %maximum_multiply_fusion = f32[1024,1176]{1,0:T(8,128)} fusion(f32[1024,536]{1,0:T(8,128)S(1)} %slice_select_fusion, f32[1024,640]{1,0:T(8,128)S(1)} %broadcast_select_fusion), kind=kLoop, calls=%fused_computation | loop fusion | flops 2408448 | bytes 9633792 | tf_op jit(solution)/shard_map/mul | solution.py:146
  81.5 10.5 %all-to-all-done.1 = f32[32,32,512]{2,1,0:T(8,128)} async-done(((f32[32,32,512]{2,1,0:T(8,128)}), f32[32,32,512]{2,1,0:T(8,128)}, u32[]{:S(2)}, u32[]{:S(2)}) %all-to-all-start.1) | async-done | bytes 2097184 | tf_op jit(solution)/shard_map/all_to_all | solution.py:123
  92.0 6.6 %all-to-all-start.3 = ((f32[32,32,512]{2,1,0:T(8,128)}), f32[32,32,512]{2,1,0:T(8,128)S(1)}, u32[]{:S(2)}, u32[]{:S(2)}) async-start(f32[32,32,512]{2,1,0:T(8,128)} %bitcast.29), calls=%async_computation.3 | async-start | bytes 4194304 | tf_op jit(solution)/shard_map/all_to_all | solution.py:123
  98.6 7.6 %fusion.4 = f32[1176,512]{1,0:T(8,128)S(1)} fusion(f32[1024,1176]{1,0:T(8,128)} %maximum_multiply_fusion, f32[1024,512]{1,0:T(8,128)} %bitcast.8), kind=kOutput, calls=%fused_computation.25 | convolution fusion | flops 3699376128 | bytes 9322496 | tf_op jit(solution)/shard_map/dot_general | solution.py:106
  106.3 2.7 %slice_add_fusion.5 = (f32[1176,256]{1,0:T(8,128)}, f32[1176,256]{1,0:T(8,128)}) fusion(f32[1176,512]{1,0:T(8,128)S(1)} %fusion.4, f32[640,256]{1,0:T(8,128)S(1)} %collective-permute-done.1, f32[536,256]{1,0:T(8,128)} %collective-permute-done.2), kind=kLoop, calls=%fused_computation.10 | loop fusion | flops 602112 | bytes 6021120 | tf_op jit(solution)/shard_map/add | solution.py:158
  109.0 3.1 %collective-permute-start.3 = (f32[1176,256]{1,0:T(8,128)}, f32[1176,256]{1,0:T(8,128)S(1)}, u32[]{:S(2)}, u32[]{:S(2)}) collective-permute-start(f32[1176,256]{1,0:T(8,128)} %get-tuple-element.39), channel_id=1, source_target_pairs={{0,2},{2,4},{4,6},{6,8},{8,10},{10,12},{12,14},{14,0},{1,3},{3,5},... | collective-permute-start | bytes 3612680 | tf_op jit(solution)/shard_map/ppermute | solution.py:150
  112.1 12.8 %all-to-all-done.3 = f32[32,32,512]{2,1,0:T(8,128)S(1)} async-done(((f32[32,32,512]{2,1,0:T(8,128)}), f32[32,32,512]{2,1,0:T(8,128)S(1)}, u32[]{:S(2)}, u32[]{:S(2)}) %all-to-all-start.3) | async-done | bytes 2097184 | tf_op jit(solution)/shard_map/all_to_all | solution.py:123
  124.9 7.3 %all-to-all-start.4 = ((f32[32,32,512]{2,1,0:T(8,128)}), f32[32,32,512]{2,1,0:T(8,128)}, u32[]{:S(2)}, u32[]{:S(2)}) async-start(f32[32,32,512]{2,1,0:T(8,128)} %bitcast.28), calls=%async_computation.4 | async-start | bytes 4194304 | tf_op jit(solution)/shard_map/all_to_all | solution.py:123
  132.2 6.9 %fusion.5 = f32[1176,512]{1,0:T(8,128)S(1)} fusion(f32[1024,1176]{1,0:T(8,128)} %maximum_multiply_fusion, f32[1024,512]{1,0:T(8,128)S(1)} %bitcast.27), kind=kOutput, calls=%fused_computation.26 | convolution fusion | flops 3699376128 | bytes 9322496 | tf_op jit(solution)/shard_map/dot_general | solution.py:106
  139.1 2.8 %collective-permute-done.6 = f32[1176,256]{1,0:T(8,128)} collective-permute-done((f32[1176,256]{1,0:T(8,128)}, f32[1176,256]{1,0:T(8,128)}, u32[]{:S(2)}, u32[]{:S(2)}) %collective-permute-start.6) | collective-permute-done | bytes 1204256 | tf_op jit(solution)/shard_map/ppermute | solution.py:151
  141.9 2.6 %slice_add_fusion.4 = (f32[1176,256]{1,0:T(8,128)}, f32[1176,256]{1,0:T(8,128)S(1)}) fusion(f32[1176,256]{1,0:T(8,128)S(1)} %collective-permute-done.3, f32[1176,512]{1,0:T(8,128)S(1)} %fusion.5, f32[1176,256]{1,0:T(8,128)} %collective-permute-done.6), kind=kLoop, calls=%fused_computation.9 | loop fusion | flops 602112 | bytes 7225344 | tf_op jit(solution)/shard_map/add | solution.py:158
  144.5 0.3 collective-permute-start.4
  144.9 1.7 collective-permute-start.7
  146.6 12.0 %all-to-all-done.4 = f32[32,32,512]{2,1,0:T(8,128)} async-done(((f32[32,32,512]{2,1,0:T(8,128)}), f32[32,32,512]{2,1,0:T(8,128)}, u32[]{:S(2)}, u32[]{:S(2)}) %all-to-all-start.4) | async-done | bytes 2097184 | tf_op jit(solution)/shard_map/all_to_all | solution.py:123
  158.6 7.7 %fusion.6 = f32[1176,512]{1,0:T(8,128)S(1)} fusion(f32[1024,1176]{1,0:T(8,128)} %maximum_multiply_fusion, f32[1024,512]{1,0:T(8,128)} %bitcast.11), kind=kOutput, calls=%fused_computation.27 | convolution fusion | flops 3699376128 | bytes 9322496 | tf_op jit(solution)/shard_map/dot_general | solution.py:106
  166.4 5.8 %collective-permute-done.4 = f32[1176,256]{1,0:T(8,128)S(1)} collective-permute-done((f32[1176,256]{1,0:T(8,128)}, f32[1176,256]{1,0:T(8,128)S(1)}, u32[]{:S(2)}, u32[]{:S(2)}) %collective-permute-start.4) | collective-permute-done | bytes 1204256 | tf_op jit(solution)/shard_map/ppermute | solution.py:150
  172.2 2.3 collective-permute-done.7
  174.5 1.7 slice_add_fusion.3
  176.1 0.5 collective-permute-start.5
  176.6 1.6 collective-permute-start.8
  178.2 22.4 %all_to_all.30 = f32[32,32,256]{2,1,0:T(8,128)S(1)} all-to-all(f32[32,32,256]{2,1,0:T(8,128)S(1)} %bitcast.33), channel_id=1, replica_groups=mesh['x'=4,'yh'=2,'yl'=2,'z'=8,'c'=2] {'x','yh','yl','c'}, dimensions={0} | all-to-all | bytes 2097152 | tf_op jit(solution)/shard_map/all_to_all | solution.py:123
  200.7 2.9 %collective-permute-done.5 = f32[1176,256]{1,0:T(8,128)S(1)} collective-permute-done((f32[1176,256]{1,0:T(8,128)S(1)}, f32[1176,256]{1,0:T(8,128)S(1)}, u32[]{:S(2)}, u32[]{:S(2)}) %collective-permute-start.5) | collective-permute-done | bytes 1204256 | tf_op jit(solution)/shard_map/ppermute | solution.py:159
  203.6 1.6 collective-permute-done.8
  205.2 4.3 %fusion = f32[1176,256]{1,0:T(8,128)S(1)} fusion(f32[1176,256]{1,0:T(8,128)S(1)} %collective-permute-done.8, f32[1176,256]{1,0:T(8,128)S(1)} %collective-permute-done.5, f32[1024,1176]{1,0:T(8,128)S(1)} %bitcast.25, f32[1024,256]{1,0:T(8,128)S(1)} %bitcast.34), kind=kOutput, calls=%fused_computation.2 | convolution fusion | flops 1850290176 | bytes 9478144 | tf_op jit(solution)/shard_map/dot_general | solution.py:106
  209.5 0.1 reshape.50
  209.7 22.2 %all_to_all.31 = f32[8,147,256]{2,1,0:T(8,128)S(1)} all-to-all(f32[8,147,256]{2,1,0:T(8,128)S(1)} %reshape.50), channel_id=1, replica_groups=mesh['x'=4,'yh'=2,'yl'=2,'z'=8,'c'=2] {'x','yh'}, dimensions={0} | all-to-all | bytes 2408448 | tf_op jit(solution)/shard_map/all_to_all | solution.py:162
  231.9 0.4 copy.9
  232.4 1.5 copy.10
  (19 shorter events, 0.1 us)
Async XLA Ops:
  3.0 52.4 %all-to-all-start = ((f32[32,32,896]{2,1,0:T(8,128)}), f32[32,32,896]{2,1,0:T(8,128)}, u32[]{:S(2)}, u32[]{:S(2)}) async-start(f32[32,32,896]{2,1,0:T(8,128)} %bitcast.26), calls=%async_computation | async-start | bytes 7340032 | tf_op jit(solution)/shard_map/all_to_all | solution.py:123
  10.7 2.1 copy-start.1
  10.7 2.1 copy-start.2
  13.3 3.5 %copy-start.3 = (s32[2]{0:T(128)S(1)}, s32[2]{0:T(128)}, u32[]{:S(2)}) copy-start(s32[2]{0:T(128)} %constant.73.clone) | copy-start | bytes 28
  57.3 10.8 %collective-permute-start = (f32[1024,640]{1,0:T(8,128)S(1)}, f32[1024,640]{1,0:T(8,128)}, u32[]{:S(2)}, u32[]{:S(2)}) collective-permute-start(f32[1024,640]{1,0:T(8,128)S(1)} %slice.27.amps_ref), channel_id=1, source_target_pairs={{0,1},{1,0},{2,3},{3,2},{4,5},{5,4},{6,7},{7,6},{8,9},{9,8},{10,11... | collective-permute-start | bytes 7864328 | tf_op jit(solution)/shard_map/ppermute | solution.py:135
  57.4 34.6 %all-to-all-start.1 = ((f32[32,32,512]{2,1,0:T(8,128)}), f32[32,32,512]{2,1,0:T(8,128)}, u32[]{:S(2)}, u32[]{:S(2)}) async-start(f32[32,32,512]{2,1,0:T(8,128)} %bitcast.30), calls=%async_computation.1 | async-start | bytes 4194304 | tf_op jit(solution)/shard_map/all_to_all | solution.py:123
  73.2 25.4 %collective-permute-start.2 = (f32[536,256]{1,0:T(8,128)}, f32[536,256]{1,0:T(8,128)}, u32[]{:S(2)}, u32[]{:S(2)}) collective-permute-start(f32[536,256]{1,0:T(8,128)} %slice_select_fusion.1), channel_id=1, source_target_pairs={{0,14},{2,0},{4,2},{6,4},{8,6},{10,8},{12,10},{14,12},{1,15},{3,1}... | collective-permute-start | bytes 1646600 | tf_op jit(solution)/shard_map/ppermute | solution.py:151
  73.3 25.3 %collective-permute-start.1 = (f32[640,256]{1,0:T(8,128)}, f32[640,256]{1,0:T(8,128)S(1)}, u32[]{:S(2)}, u32[]{:S(2)}) collective-permute-start(f32[640,256]{1,0:T(8,128)} %broadcast_select_fusion.1), channel_id=1, source_target_pairs={{0,2},{2,4},{4,6},{6,8},{8,10},{10,12},{12,14},{14,0},{1,3},{3,5},... | collective-permute-start | bytes 1966088 | tf_op jit(solution)/shard_map/ppermute | solution.py:150
  92.0 33.0 %all-to-all-start.3 = ((f32[32,32,512]{2,1,0:T(8,128)}), f32[32,32,512]{2,1,0:T(8,128)S(1)}, u32[]{:S(2)}, u32[]{:S(2)}) async-start(f32[32,32,512]{2,1,0:T(8,128)} %bitcast.29), calls=%async_computation.3 | async-start | bytes 4194304 | tf_op jit(solution)/shard_map/all_to_all | solution.py:123
  109.0 30.1 %collective-permute-start.3 = (f32[1176,256]{1,0:T(8,128)}, f32[1176,256]{1,0:T(8,128)S(1)}, u32[]{:S(2)}, u32[]{:S(2)}) collective-permute-start(f32[1176,256]{1,0:T(8,128)} %get-tuple-element.39), channel_id=1, source_target_pairs={{0,2},{2,4},{4,6},{6,8},{8,10},{10,12},{12,14},{14,0},{1,3},{3,5},... | collective-permute-start | bytes 3612680 | tf_op jit(solution)/shard_map/ppermute | solution.py:150
  112.1 29.8 %collective-permute-start.6 = (f32[1176,256]{1,0:T(8,128)}, f32[1176,256]{1,0:T(8,128)}, u32[]{:S(2)}, u32[]{:S(2)}) collective-permute-start(f32[1176,256]{1,0:T(8,128)} %get-tuple-element.40), channel_id=1, source_target_pairs={{0,14},{2,0},{4,2},{6,4},{8,6},{10,8},{12,10},{14,12},{1,15},{3,1}... | collective-permute-start | bytes 3612680 | tf_op jit(solution)/shard_map/ppermute | solution.py:151
  124.9 33.6 %all-to-all-start.4 = ((f32[32,32,512]{2,1,0:T(8,128)}), f32[32,32,512]{2,1,0:T(8,128)}, u32[]{:S(2)}, u32[]{:S(2)}) async-start(f32[32,32,512]{2,1,0:T(8,128)} %bitcast.28), calls=%async_computation.4 | async-start | bytes 4194304 | tf_op jit(solution)/shard_map/all_to_all | solution.py:123
  144.5 27.6 %collective-permute-start.4 = (f32[1176,256]{1,0:T(8,128)}, f32[1176,256]{1,0:T(8,128)S(1)}, u32[]{:S(2)}, u32[]{:S(2)}) collective-permute-start(f32[1176,256]{1,0:T(8,128)} %get-tuple-element.37), channel_id=1, source_target_pairs={{0,2},{2,4},{4,6},{6,8},{8,10},{10,12},{12,14},{14,0},{1,3},{3,5},... | collective-permute-start | bytes 3612680 | tf_op jit(solution)/shard_map/ppermute | solution.py:150
  144.9 29.6 %collective-permute-start.7 = (f32[1176,256]{1,0:T(8,128)S(1)}, f32[1176,256]{1,0:T(8,128)}, u32[]{:S(2)}, u32[]{:S(2)}) collective-permute-start(f32[1176,256]{1,0:T(8,128)S(1)} %get-tuple-element.38), channel_id=1, source_target_pairs={{0,14},{2,0},{4,2},{6,4},{8,6},{10,8},{12,10},{14,12},{1,15},{3,1}... | collective-permute-start | bytes 3612680 | tf_op jit(solution)/shard_map/ppermute | solution.py:151
  158.6 46.7 %slice-start = ((s8[5242880]{0:T(1024)(128)(4,1)}), s8[4194304]{0:T(1024)(128)(4,1)S(1)}, s32[]{:S(2)}) async-start(s8[5242880]{0:T(1024)(128)(4,1)} %bitcast.24), calls=%async_computation.6 | async-start | bytes 8388608
  158.6 46.7 %slice-start.1 = ((s8[5242880]{0:T(1024)(128)(4,1)}), s8[1048576]{0:T(1024)(128)(4,1)S(1)}, s32[]{:S(2)}) async-start(s8[5242880]{0:T(1024)(128)(4,1)} %bitcast.24), calls=%async_computation.7 | async-start | bytes 2097152
  166.3 11.9 %copy-start = (f32[8,4,32,256]{3,2,1,0:T(8,128)S(1)}, f32[8,4,32,256]{3,2,1,0:T(8,128)}, u32[]{:S(2)}) copy-start(f32[8,4,32,256]{3,2,1,0:T(8,128)} %pack.9) | copy-start | bytes 3145732
  176.1 27.5 %collective-permute-start.5 = (f32[1176,256]{1,0:T(8,128)S(1)}, f32[1176,256]{1,0:T(8,128)S(1)}, u32[]{:S(2)}, u32[]{:S(2)}) collective-permute-start(f32[1176,256]{1,0:T(8,128)S(1)} %get-tuple-element.35), channel_id=1, source_target_pairs={{0,2},{2,4},{4,6},{6,8},{8,10},{10,12},{12,14},{14,0},{1,3},{3,5},... | collective-permute-start | bytes 3612680 | tf_op jit(solution)/shard_map/ppermute | solution.py:159
  176.6 28.6 %collective-permute-start.8 = (f32[1176,256]{1,0:T(8,128)S(1)}, f32[1176,256]{1,0:T(8,128)S(1)}, u32[]{:S(2)}, u32[]{:S(2)}) collective-permute-start(f32[1176,256]{1,0:T(8,128)S(1)} %get-tuple-element.36), channel_id=1, source_target_pairs={{0,14},{2,0},{4,2},{6,4},{8,6},{10,8},{12,10},{14,12},{1,15},{3,1}... | collective-permute-start | bytes 3612680 | tf_op jit(solution)/shard_map/ppermute | solution.py:160

commit v3 on v2

--- a/solution.py
+++ b/solution.py
@@ -16,32 +16,34 @@
 
 
 def pack_kernel(n, blocks_ref, *refs):
+    out_ref = refs[n] if len(refs) == n + 1 else refs[n + 1]
     for k in range(n):
-        for c in range(2):
-            for s in range(8):
-                start = c * 2048 + s * 256
-                refs[-1 if len(refs) == n + 1 else n + 1][
-                    s, c, :, k * 256 : (k + 1) * 256
-                ] = refs[k][:, start : start + 256]
+        for s in range(8):
+            piece = refs[k][:, s * 256 : (s + 1) * 256]
+            out_ref[s, 0, :, k * 256 : (k + 1) * 256] = piece
     if len(refs) == n + 1:
         return
-    amps_ref, out_ref, wide = refs[n:]
+    amps_ref, wide = refs[n], refs[n + 2]
     wide[:, 1152:] = jnp.zeros((wide.shape[0], 128), jnp.float32)
     wide[:, :IJ] = amps_ref[...]
     for c in range(2):
-        for s in range(8):
-            out_ref[s, c, :, n * 256 :] = wide[:, c * HALF : (c + 1) * HALF]
+
+        @pl.when(pl.program_id(1) == c)
+        def _(c=c):
+            for s in range(8):
+                out_ref[s, 0, :, n * 256 :] = wide[:, c * HALF : (c + 1) * HALF]
 
 
 def pack(integrals, blocks, n, amplitudes=None):
     rows = integrals.shape[0]
     width = n * 256 + (0 if amplitudes is None else HALF)
     specs = [
-        pl.BlockSpec((rows, 4096), lambda y, b, k=k: (0, y * NZ + b[k])) for k in range(n)
+        pl.BlockSpec((rows, 2048), lambda y, c, b, k=k: (0, (y * NZ + b[k]) * 2 + c))
+        for k in range(n)
     ]
     extra, scratch = [], []
     if amplitudes is not None:
-        specs.append(pl.BlockSpec((rows, IJ), lambda y, b: (0, 0)))
+        specs.append(pl.BlockSpec((rows, IJ), lambda y, c, b: (0, 0)))
         extra.append(amplitudes)
         scratch.append(pltpu.VMEM((rows, 2 * HALF), jnp.float32))
     out = pl.pallas_call(
@@ -49,9 +51,9 @@
         out_shape=jax.ShapeDtypeStruct((8, 4, rows, width), jnp.float32),
         grid_spec=pltpu.PrefetchScalarGridSpec(
             num_scalar_prefetch=1,
-            grid=(2,),
+            grid=(2, 2),
             in_specs=specs,
-            out_specs=pl.BlockSpec((8, 2, rows, width), lambda y, b: (0, y, 0, 0)),
+            out_specs=pl.BlockSpec((8, 1, rows, width), lambda y, c, b: (0, y * 2 + c, 0, 0)),
             scratch_shapes=scratch,
         ),
         compiler_params=BIG,
@@ -158,7 +160,8 @@
         right, left = right + product[:, :256], left + product[:, 256:]
     right = lax.ppermute(right, "z", up)
     left = lax.ppermute(left, "z", down)
-    total = (contract(amps, swap(sent[4])) + right + left).reshape(8, ROWS, 256)
+    product = lax.optimization_barrier(contract(amps, swap(sent[4])))
+    total = (product + right + left).reshape(8, ROWS, 256)
     got = lax.all_to_all(total, ("x", "yh"), split_axis=0, concat_axis=0, tiled=True)
     return got.transpose(1, 0, 2).reshape(ROWS, 8 * 256)
 

time: 237 us -> 239 us (level)
  blocking collectives: 44.7 us -> 23.1 us
  starting transfers between devices: 40.3 us -> 46.7 us
  Pallas kernels: 21 us -> 26.9 us
  waiting for transfers between devices: 82.2 us -> 87.3 us
  matrix products: 26.5 us -> 29 us
  other arithmetic: 15 us -> 17.5 us
    all_to_all x1 -> x0, blocking collectives: 22.4 us -> none  [swap(): got = lax.all_to_all(sent, PLANE, split_axis=0, concat_axis=0, tiled=True)]
    ppermute x4, waiting for transfers between devices: 8.73 us -> 17.4 us  [on_device(): right = lax.ppermute(right, 'z', up)]
    all_to_all x4 -> x5, starting transfers between devices: 29.7 us -> 36.2 us  [swap(): got = lax.all_to_all(sent, PLANE, split_axis=0, concat_axis=0, tiled=True)]
    pallas_call x5, Pallas kernels: 15.3 us -> 21.2 us  [pack(): pl.pallas_call(lambda *refs: pack_kernel(n, *refs), out_shape=jax.ShapeDt...]
    all_to_all x4 -> x5, waiting for transfers between devices: 66.7 us -> 62.8 us  [swap(): got = lax.all_to_all(sent, PLANE, split_axis=0, concat_axis=0, tiled=True)]
    dot_general x4, matrix products: 26.5 us -> 29 us  [contract(): lax.dot_general(left_side, right_side, (((0,), (0,)), ((), ())), precisio...]
  transfers between devices with their start and end apart: 13 -> 14, of which waited for: 9 -> 9; matrix products, arithmetic and copies ran while one was open for 15% -> 19% of each run, Pallas kernels for 8% -> 10%
where the time goes in v3:
time: 239 us; the launch traced here: 236 us
  waiting for transfers between devices  87.3 us (37%)
  starting transfers between devices  46.7 us (20%)
  matrix products  29 us (12%)
  Pallas kernels  26.9 us (11%)
  blocking collectives  23.1 us (10%)
  other arithmetic  17.5 us (7%)
  local copies, waits for them, and re-layouts  5.04 us (2%)
    all_to_all x5, waiting for transfers between devices, swap(): got = lax.all_to_all(sent, PLANE, split_axis=0, concat_axis=0, tiled=True)  62.8 us
    all_to_all x5, starting transfers between devices, swap(): got = lax.all_to_all(sent, PLANE, split_axis=0, concat_axis=0, tiled=True)  36.2 us
    dot_general x4, matrix products, contract(): lax.dot_general(left_side, right_side, (((0,), (0,)), ((), ())), precisio...  29 us
    all_to_all x1, blocking collectives, on_device(): lax.all_to_all(total, ('x', 'yh'), split_axis=0, concat_axis=0, tiled=True)  23.1 us
    pallas_call x5, Pallas kernels, pack(): pl.pallas_call(lambda *refs: pack_kernel(n, *refs), out_shape=jax.ShapeDt...  21.2 us
    ppermute x4, waiting for transfers between devices, on_device(): right = lax.ppermute(right, 'z', up)  17.4 us
    add x3, other arithmetic, on_device(): right, left = (right + product[:, :256], left + product[:, 256:])  7.69 us
    ppermute x4, starting transfers between devices, on_device(): right = lax.ppermute(right, 'z', up)  7.46 us
  transfers between devices with their start and end apart: 14, of which 9 were waited for; matrix products, arithmetic and copies ran while one was open for 19% of the time, Pallas kernels for 10%

profile of v3, /device:TPU:102, one launch (start us, length us, event | category | flops | bytes accessed | tf_op | source)
XLA Modules:
  0.0 235.7 jit_solution(9422104431367273942)
XLA Ops:
  0.0 4.1 %pack.5 = f32[8,4,32,896]{3,2,1,0:T(8,128)} custom-call(s32[1]{0:T(128)S(6)} %select_n.49.refs_0_, f32[32,65536]{1,0:T(8,128)} %refs_1_.9, f32[32,1176]{1,0:T(8,128)} %refs_2_.4), custom_call_target="tpu_custom_call" | custom-call | bytes 7340032 | tf_op jit(solution)/shard_map/pack/pallas_call | solution.py:49
  4.1 7.7 %all-to-all-start = ((f32[32,32,896]{2,1,0:T(8,128)}), f32[32,32,896]{2,1,0:T(8,128)}, u32[]{:S(2)}, u32[]{:S(2)}) async-start(f32[32,32,896]{2,1,0:T(8,128)} %bitcast.24), calls=%async_computation | async-start | bytes 7340032 | tf_op jit(solution)/shard_map/all_to_all | solution.py:125
  11.8 3.4 %pack.9 = f32[8,4,32,256]{3,2,1,0:T(8,128)} custom-call(s32[1]{0:T(128)S(6)} %select_n.53.refs_0_, f32[32,65536]{1,0:T(8,128)} %refs_1_.9), custom_call_target="tpu_custom_call" | custom-call | bytes 2097152 | tf_op jit(solution)/shard_map/pack/pallas_call | solution.py:49
  15.2 0.6 and_select_fusion
  15.8 4.7 %pack.8 = f32[8,4,32,512]{3,2,1,0:T(8,128)} custom-call(s32[2]{0:T(128)} %get-tuple-element.41.refs_0_, f32[32,65536]{1,0:T(8,128)} %refs_1_.9, f32[32,65536]{1,0:T(8,128)} %refs_1_.9), custom_call_target="tpu_custom_call" | custom-call | bytes 4194304 | tf_op jit(solution)/shard_map/pack/pallas_call | solution.py:49
  20.5 0.5 and_select_fusion.2.refs_0_
  21.0 4.5 %pack.6 = f32[8,4,32,512]{3,2,1,0:T(8,128)} custom-call(s32[2]{0:T(128)} %and_select_fusion.2.refs_0_, f32[32,65536]{1,0:T(8,128)} %refs_1_.9, f32[32,65536]{1,0:T(8,128)} %refs_1_.9), custom_call_target="tpu_custom_call" | custom-call | bytes 4194304 | tf_op jit(solution)/shard_map/pack/pallas_call | solution.py:49
  25.5 4.5 %pack.7 = f32[8,4,32,512]{3,2,1,0:T(8,128)} custom-call(s32[2]{0:T(128)} %get-tuple-element.42.refs_0_, f32[32,65536]{1,0:T(8,128)} %refs_1_.9, f32[32,65536]{1,0:T(8,128)} %refs_1_.9), custom_call_target="tpu_custom_call" | custom-call | bytes 4194304 | tf_op jit(solution)/shard_map/pack/pallas_call | solution.py:49
  30.0 26.5 %all-to-all-done = f32[32,32,896]{2,1,0:T(8,128)} async-done(((f32[32,32,896]{2,1,0:T(8,128)}), f32[32,32,896]{2,1,0:T(8,128)}, u32[]{:S(2)}, u32[]{:S(2)}) %all-to-all-start) | async-done | bytes 3670048 | tf_op jit(solution)/shard_map/all_to_all | solution.py:125
  56.5 1.9 slice.27.amps_ref
  58.5 8.2 %all-to-all-start.1 = ((f32[32,32,512]{2,1,0:T(8,128)}), f32[32,32,512]{2,1,0:T(8,128)}, u32[]{:S(2)}, u32[]{:S(2)}) async-start(f32[32,32,512]{2,1,0:T(8,128)} %bitcast.28), calls=%async_computation.1 | async-start | bytes 4194304 | tf_op jit(solution)/shard_map/all_to_all | solution.py:125
  66.7 2.5 %first.2 = f32[640,256]{1,0:T(8,128)S(1)} custom-call(f32[1024,640]{1,0:T(8,128)S(1)} %slice.27.amps_ref, f32[1024,896]{1,0:T(8,128)} %bitcast.2.v_ref), custom_call_target="tpu_custom_call" | custom-call | flops 1006632960 | bytes 4325376 | tf_op jit(solution)/shard_map/first/pallas_call | solution.py:88
  69.2 3.3 %first.3 = f32[640,256]{1,0:T(8,128)S(1)} custom-call(f32[1024,640]{1,0:T(8,128)} %collective-permute-done.amps_ref, f32[1024,896]{1,0:T(8,128)} %bitcast.2.v_ref), custom_call_target="tpu_custom_call" | custom-call | flops 1006632960 | bytes 4325376 | tf_op jit(solution)/shard_map/first/pallas_call | solution.py:88
  72.4 0.9 slice_select_fusion.1
  73.3 0.9 broadcast_select_fusion.1
  74.3 3.1 %collective-permute-start.1 = (f32[640,256]{1,0:T(8,128)}, f32[640,256]{1,0:T(8,128)S(1)}, u32[]{:S(2)}, u32[]{:S(2)}) collective-permute-start(f32[640,256]{1,0:T(8,128)} %broadcast_select_fusion.1), channel_id=1, source_target_pairs={{0,2},{2,4},{4,6},{6,8},{8,10},{10,12},{12,14},{14,0},{1,3},{3,5},... | collective-permute-start | bytes 1966088 | tf_op jit(solution)/shard_map/ppermute | solution.py:152
  77.5 2.0 slice_select_fusion
  79.5 0.3 broadcast_select_fusion
  79.8 2.8 %maximum_multiply_fusion = f32[1024,1176]{1,0:T(8,128)} fusion(f32[1024,536]{1,0:T(8,128)S(1)} %slice_select_fusion, f32[1024,640]{1,0:T(8,128)S(1)} %broadcast_select_fusion), kind=kLoop, calls=%fused_computation | loop fusion | flops 2408448 | bytes 9633792 | tf_op jit(solution)/shard_map/mul | solution.py:148
  82.5 10.5 %all-to-all-done.1 = f32[32,32,512]{2,1,0:T(8,128)} async-done(((f32[32,32,512]{2,1,0:T(8,128)}), f32[32,32,512]{2,1,0:T(8,128)}, u32[]{:S(2)}, u32[]{:S(2)}) %all-to-all-start.1) | async-done | bytes 2097184 | tf_op jit(solution)/shard_map/all_to_all | solution.py:125
  93.0 6.6 %all-to-all-start.3 = ((f32[32,32,512]{2,1,0:T(8,128)}), f32[32,32,512]{2,1,0:T(8,128)S(1)}, u32[]{:S(2)}, u32[]{:S(2)}) async-start(f32[32,32,512]{2,1,0:T(8,128)} %bitcast.27), calls=%async_computation.3 | async-start | bytes 4194304 | tf_op jit(solution)/shard_map/all_to_all | solution.py:125
  99.7 7.6 %fusion.4 = f32[1176,512]{1,0:T(8,128)S(1)} fusion(f32[1024,1176]{1,0:T(8,128)} %maximum_multiply_fusion, f32[1024,512]{1,0:T(8,128)} %bitcast.8), kind=kOutput, calls=%fused_computation.25 | convolution fusion | flops 3699376128 | bytes 9322496 | tf_op jit(solution)/shard_map/dot_general | solution.py:108
  107.3 2.7 %slice_add_fusion.5 = (f32[1176,256]{1,0:T(8,128)}, f32[1176,256]{1,0:T(8,128)}) fusion(f32[1176,512]{1,0:T(8,128)S(1)} %fusion.4, f32[640,256]{1,0:T(8,128)S(1)} %collective-permute-done.1, f32[536,256]{1,0:T(8,128)} %collective-permute-done.2), kind=kLoop, calls=%fused_computation.8 | loop fusion | flops 602112 | bytes 6021120 | tf_op jit(solution)/shard_map/add | solution.py:160
  110.1 3.1 %collective-permute-start.3 = (f32[1176,256]{1,0:T(8,128)}, f32[1176,256]{1,0:T(8,128)S(1)}, u32[]{:S(2)}, u32[]{:S(2)}) collective-permute-start(f32[1176,256]{1,0:T(8,128)} %get-tuple-element.39), channel_id=1, source_target_pairs={{0,2},{2,4},{4,6},{6,8},{8,10},{10,12},{12,14},{14,0},{1,3},{3,5},... | collective-permute-start | bytes 3612680 | tf_op jit(solution)/shard_map/ppermute | solution.py:152
  113.2 12.8 %all-to-all-done.3 = f32[32,32,512]{2,1,0:T(8,128)S(1)} async-done(((f32[32,32,512]{2,1,0:T(8,128)}), f32[32,32,512]{2,1,0:T(8,128)S(1)}, u32[]{:S(2)}, u32[]{:S(2)}) %all-to-all-start.3) | async-done | bytes 2097184 | tf_op jit(solution)/shard_map/all_to_all | solution.py:125
  126.0 7.3 %all-to-all-start.4 = ((f32[32,32,512]{2,1,0:T(8,128)}), f32[32,32,512]{2,1,0:T(8,128)}, u32[]{:S(2)}, u32[]{:S(2)}) async-start(f32[32,32,512]{2,1,0:T(8,128)} %bitcast.26), calls=%async_computation.4 | async-start | bytes 4194304 | tf_op jit(solution)/shard_map/all_to_all | solution.py:125
  133.3 6.9 %fusion.5 = f32[1176,512]{1,0:T(8,128)S(1)} fusion(f32[1024,1176]{1,0:T(8,128)} %maximum_multiply_fusion, f32[1024,512]{1,0:T(8,128)S(1)} %bitcast.25), kind=kOutput, calls=%fused_computation.26 | convolution fusion | flops 3699376128 | bytes 9322496 | tf_op jit(solution)/shard_map/dot_general | solution.py:108
  140.2 2.8 %collective-permute-done.6 = f32[1176,256]{1,0:T(8,128)} collective-permute-done((f32[1176,256]{1,0:T(8,128)}, f32[1176,256]{1,0:T(8,128)}, u32[]{:S(2)}, u32[]{:S(2)}) %collective-permute-start.6) | collective-permute-done | bytes 1204256 | tf_op jit(solution)/shard_map/ppermute | solution.py:153
  143.0 3.0 %slice_add_fusion.4 = (f32[1176,256]{1,0:T(8,128)}, f32[1176,256]{1,0:T(8,128)}) fusion(f32[1176,256]{1,0:T(8,128)S(1)} %collective-permute-done.3, f32[1176,512]{1,0:T(8,128)S(1)} %fusion.5, f32[1176,256]{1,0:T(8,128)} %collective-permute-done.6), kind=kLoop, calls=%fused_computation.7 | loop fusion | flops 602112 | bytes 7225344 | tf_op jit(solution)/shard_map/add | solution.py:160
  146.0 0.4 collective-permute-start.4
  146.4 1.7 collective-permute-start.7
  148.1 11.6 %all-to-all-done.4 = f32[32,32,512]{2,1,0:T(8,128)} async-done(((f32[32,32,512]{2,1,0:T(8,128)}), f32[32,32,512]{2,1,0:T(8,128)}, u32[]{:S(2)}, u32[]{:S(2)}) %all-to-all-start.4) | async-done | bytes 2097184 | tf_op jit(solution)/shard_map/all_to_all | solution.py:125
  159.7 6.5 %all-to-all-start.2 = ((f32[32,32,256]{2,1,0:T(8,128)}), f32[32,32,256]{2,1,0:T(8,128)S(1)}, u32[]{:S(2)}, u32[]{:S(2)}) async-start(f32[32,32,256]{2,1,0:T(8,128)} %bitcast.7), calls=%async_computation.2 | async-start | bytes 2097152 | tf_op jit(solution)/shard_map/all_to_all | solution.py:125
  166.2 7.6 %fusion.6 = f32[1176,512]{1,0:T(8,128)S(1)} fusion(f32[1024,1176]{1,0:T(8,128)} %maximum_multiply_fusion, f32[1024,512]{1,0:T(8,128)} %bitcast.11), kind=kOutput, calls=%fused_computation.27 | convolution fusion | flops 3699376128 | bytes 9322496 | tf_op jit(solution)/shard_map/dot_general | solution.py:108
  173.8 2.3 collective-permute-done.7
  176.1 1.9 slice_add_fusion.3
  178.0 0.8 collective-permute-start.5
  178.8 1.2 collective-permute-start.8
  180.0 1.4 all-to-all-done.2
  181.4 6.8 %fusion.3 = f32[1176,256]{1,0:T(8,128)S(1)} fusion(f32[1024,1176]{1,0:T(8,128)} %maximum_multiply_fusion, f32[1024,256]{1,0:T(8,128)S(1)} %bitcast.31), kind=kOutput, calls=%fused_computation.24 | convolution fusion | flops 1849688064 | bytes 7069696 | tf_op jit(solution)/shard_map/dot_general | solution.py:108
  188.2 17.4 %collective-permute-done.5 = f32[1176,256]{1,0:T(8,128)S(1)} collective-permute-done((f32[1176,256]{1,0:T(8,128)}, f32[1176,256]{1,0:T(8,128)S(1)}, u32[]{:S(2)}, u32[]{:S(2)}) %collective-permute-start.5) | collective-permute-done | bytes 1204256 | tf_op jit(solution)/shard_map/ppermute | solution.py:161
  205.6 1.0 copy-done
  206.6 2.0 collective-permute-done.8
  208.6 1.9 add_add_fusion
  210.5 0.1 reshape.50
  210.7 23.1 %all_to_all.30 = f32[8,147,256]{2,1,0:T(8,128)S(1)} all-to-all(f32[8,147,256]{2,1,0:T(8,128)S(1)} %reshape.50), channel_id=1, replica_groups=mesh['x'=4,'yh'=2,'yl'=2,'z'=8,'c'=2] {'x','yh'}, dimensions={0} | all-to-all | bytes 2408448 | tf_op jit(solution)/shard_map/all_to_all | solution.py:165
  233.7 0.4 copy.9
  234.2 1.5 copy.10
  (16 shorter events, 0.3 us)
Async XLA Ops:
  4.1 52.4 %all-to-all-start = ((f32[32,32,896]{2,1,0:T(8,128)}), f32[32,32,896]{2,1,0:T(8,128)}, u32[]{:S(2)}, u32[]{:S(2)}) async-start(f32[32,32,896]{2,1,0:T(8,128)} %bitcast.24), calls=%async_computation | async-start | bytes 7340032 | tf_op jit(solution)/shard_map/all_to_all | solution.py:125
  11.7 3.5 %copy-start.1 = (s32[2]{0:T(128)S(1)}, s32[2]{0:T(128)}, u32[]{:S(2)}) copy-start(s32[2]{0:T(128)} %constant.75.clone) | copy-start | bytes 28
  11.8 3.4 %copy-start.2 = (s32[2]{0:T(128)S(1)}, s32[2]{0:T(128)}, u32[]{:S(2)}) copy-start(s32[2]{0:T(128)} %constant.74.clone) | copy-start | bytes 28
  15.8 4.7 %copy-start.3 = (s32[2]{0:T(128)S(1)}, s32[2]{0:T(128)}, u32[]{:S(2)}) copy-start(s32[2]{0:T(128)} %constant.73.clone) | copy-start | bytes 28
  58.4 10.8 %collective-permute-start = (f32[1024,640]{1,0:T(8,128)S(1)}, f32[1024,640]{1,0:T(8,128)}, u32[]{:S(2)}, u32[]{:S(2)}) collective-permute-start(f32[1024,640]{1,0:T(8,128)S(1)} %slice.27.amps_ref), channel_id=1, source_target_pairs={{0,1},{1,0},{2,3},{3,2},{4,5},{5,4},{6,7},{7,6},{8,9},{9,8},{10,11... | collective-permute-start | bytes 7864328 | tf_op jit(solution)/shard_map/ppermute | solution.py:137
  58.5 34.6 %all-to-all-start.1 = ((f32[32,32,512]{2,1,0:T(8,128)}), f32[32,32,512]{2,1,0:T(8,128)}, u32[]{:S(2)}, u32[]{:S(2)}) async-start(f32[32,32,512]{2,1,0:T(8,128)} %bitcast.28), calls=%async_computation.1 | async-start | bytes 4194304 | tf_op jit(solution)/shard_map/all_to_all | solution.py:125
  74.2 25.4 %collective-permute-start.2 = (f32[536,256]{1,0:T(8,128)}, f32[536,256]{1,0:T(8,128)}, u32[]{:S(2)}, u32[]{:S(2)}) collective-permute-start(f32[536,256]{1,0:T(8,128)} %slice_select_fusion.1), channel_id=1, source_target_pairs={{0,14},{2,0},{4,2},{6,4},{8,6},{10,8},{12,10},{14,12},{1,15},{3,1}... | collective-permute-start | bytes 1646600 | tf_op jit(solution)/shard_map/ppermute | solution.py:153
  74.3 25.3 %collective-permute-start.1 = (f32[640,256]{1,0:T(8,128)}, f32[640,256]{1,0:T(8,128)S(1)}, u32[]{:S(2)}, u32[]{:S(2)}) collective-permute-start(f32[640,256]{1,0:T(8,128)} %broadcast_select_fusion.1), channel_id=1, source_target_pairs={{0,2},{2,4},{4,6},{6,8},{8,10},{10,12},{12,14},{14,0},{1,3},{3,5},... | collective-permute-start | bytes 1966088 | tf_op jit(solution)/shard_map/ppermute | solution.py:152
  93.0 33.0 %all-to-all-start.3 = ((f32[32,32,512]{2,1,0:T(8,128)}), f32[32,32,512]{2,1,0:T(8,128)S(1)}, u32[]{:S(2)}, u32[]{:S(2)}) async-start(f32[32,32,512]{2,1,0:T(8,128)} %bitcast.27), calls=%async_computation.3 | async-start | bytes 4194304 | tf_op jit(solution)/shard_map/all_to_all | solution.py:125
  110.1 30.1 %collective-permute-start.3 = (f32[1176,256]{1,0:T(8,128)}, f32[1176,256]{1,0:T(8,128)S(1)}, u32[]{:S(2)}, u32[]{:S(2)}) collective-permute-start(f32[1176,256]{1,0:T(8,128)} %get-tuple-element.39), channel_id=1, source_target_pairs={{0,2},{2,4},{4,6},{6,8},{8,10},{10,12},{12,14},{14,0},{1,3},{3,5},... | collective-permute-start | bytes 3612680 | tf_op jit(solution)/shard_map/ppermute | solution.py:152
  113.2 29.8 %collective-permute-start.6 = (f32[1176,256]{1,0:T(8,128)}, f32[1176,256]{1,0:T(8,128)}, u32[]{:S(2)}, u32[]{:S(2)}) collective-permute-start(f32[1176,256]{1,0:T(8,128)} %get-tuple-element.40), channel_id=1, source_target_pairs={{0,14},{2,0},{4,2},{6,4},{8,6},{10,8},{12,10},{14,12},{1,15},{3,1}... | collective-permute-start | bytes 3612680 | tf_op jit(solution)/shard_map/ppermute | solution.py:153
  126.0 33.7 %all-to-all-start.4 = ((f32[32,32,512]{2,1,0:T(8,128)}), f32[32,32,512]{2,1,0:T(8,128)}, u32[]{:S(2)}, u32[]{:S(2)}) async-start(f32[32,32,512]{2,1,0:T(8,128)} %bitcast.26), calls=%async_computation.4 | async-start | bytes 4194304 | tf_op jit(solution)/shard_map/all_to_all | solution.py:125
  146.0 27.8 %collective-permute-start.4 = (f32[1176,256]{1,0:T(8,128)}, f32[1176,256]{1,0:T(8,128)S(1)}, u32[]{:S(2)}, u32[]{:S(2)}) collective-permute-start(f32[1176,256]{1,0:T(8,128)} %get-tuple-element.37), channel_id=1, source_target_pairs={{0,2},{2,4},{4,6},{6,8},{8,10},{10,12},{12,14},{14,0},{1,3},{3,5},... | collective-permute-start | bytes 3612680 | tf_op jit(solution)/shard_map/ppermute | solution.py:152
  146.4 29.7 %collective-permute-start.7 = (f32[1176,256]{1,0:T(8,128)}, f32[1176,256]{1,0:T(8,128)S(1)}, u32[]{:S(2)}, u32[]{:S(2)}) collective-permute-start(f32[1176,256]{1,0:T(8,128)} %get-tuple-element.38), channel_id=1, source_target_pairs={{0,14},{2,0},{4,2},{6,4},{8,6},{10,8},{12,10},{14,12},{1,15},{3,1}... | collective-permute-start | bytes 3612680 | tf_op jit(solution)/shard_map/ppermute | solution.py:153
  159.7 21.8 %all-to-all-start.2 = ((f32[32,32,256]{2,1,0:T(8,128)}), f32[32,32,256]{2,1,0:T(8,128)S(1)}, u32[]{:S(2)}, u32[]{:S(2)}) async-start(f32[32,32,256]{2,1,0:T(8,128)} %bitcast.7), calls=%async_computation.2 | async-start | bytes 2097152 | tf_op jit(solution)/shard_map/all_to_all | solution.py:125
  178.0 27.6 %collective-permute-start.5 = (f32[1176,256]{1,0:T(8,128)}, f32[1176,256]{1,0:T(8,128)S(1)}, u32[]{:S(2)}, u32[]{:S(2)}) collective-permute-start(f32[1176,256]{1,0:T(8,128)} %get-tuple-element.35), channel_id=1, source_target_pairs={{0,2},{2,4},{4,6},{6,8},{8,10},{10,12},{12,14},{14,0},{1,3},{3,5},... | collective-permute-start | bytes 3612680 | tf_op jit(solution)/shard_map/ppermute | solution.py:161
  178.8 29.8 %collective-permute-start.8 = (f32[1176,256]{1,0:T(8,128)}, f32[1176,256]{1,0:T(8,128)}, u32[]{:S(2)}, u32[]{:S(2)}) collective-permute-start(f32[1176,256]{1,0:T(8,128)} %get-tuple-element.36), channel_id=1, source_target_pairs={{0,14},{2,0},{4,2},{6,4},{8,6},{10,8},{12,10},{14,12},{1,15},{3,1}... | collective-permute-start | bytes 3612680 | tf_op jit(solution)/shard_map/ppermute | solution.py:162
  205.6 1.0 copy-start
